TPU v7x, 256 devices: a whole 4x4x8 slice. The times are simulated.
256 devices in a mesh: win: 32 (over y, z), pos: 8 (over x, core).
Axes of the slice: x: 4, y: 4, z: 8, core: 2. Of those that a mesh axis runs over, the one named last changes fastest.
Arguments:
- tokens: bfloat16 [256, 128, 2560], P('win'), may hold values from -6 to 6
- keep_index: int32 [256, 128], P('win'), may hold values from 0 to 255, as said below
- norm_gain: float32 [2560], replicated, may hold values from 0.5 to 1.5
- w_qkv: bfloat16 [3, 2560, 2560], P(None, 'pos'), may hold values from -0.125 to 0.125
- w_out: bfloat16 [2560, 2560], P('pos'), may hold values from -1 to 1
Outputs:
- mixed: bfloat16 [256, 128, 2560], P('win', 'pos')
Inputs may be any that keep to these rules, and one draw needn't show every extreme that they name: keep_index[w, j] is 2 j or 2 j + 1: each window keeps exactly one position of every aligned pair of positions.
All inputs are finite; a program needn't handle non-finite values.
Results may differ from a plain program's by a relative error of at most 0.019.
Values may be sent and summed in bfloat16 or wider, within the bound.
No kernel may reach another device: no remote copies, remote signals or barrier semaphores. Data moves between devices by JAX's collectives and lax.ppermute only.
A program may use at most 128 MiB of HBM per device.

v0:
```python
import math

import jax
import jax.numpy as jnp
from jax import lax
from jax.sharding import PartitionSpec as P

D = 2560
HEADS = 16
POSITIONS = 256


NORM_EPSILON = 1e-05


def local(tokens, keep_index, norm_gain, w_qkv, w_out):
    win_count = lax.axis_size("win")
    pos_count = lax.axis_size("pos")
    local_windows, keep_count, model_width = tokens.shape
    group_width = w_qkv.shape[1]
    head_dim = D // HEADS
    head_local = group_width // head_dim
    per_device = POSITIONS // win_count
    all_windows = local_windows * win_count
    kept_rows = keep_count // pos_count
    score_scale = 1.0 / math.sqrt(head_dim)
    activations = tokens.astype(jnp.float32)
    average = jnp.mean(activations, axis=-1, keepdims=True)
    centered = activations - average
    variance = jnp.mean(centered * centered, axis=-1, keepdims=True)
    normed = (centered * lax.rsqrt(variance + NORM_EPSILON) * norm_gain).astype(jnp.bfloat16)
    projected = lax.dot_general(
        normed.reshape(local_windows * keep_count, model_width),
        w_qkv.reshape(3 * group_width, model_width),
        (((1,), (1,)), ((), ())),
        preferred_element_type=jnp.float32,
    )
    projected = projected.astype(jnp.bfloat16).reshape(local_windows, keep_count, 3 * group_width)
    places = jnp.arange(POSITIONS, dtype=jnp.int32)
    matches = keep_index[:, None, :] == places[None, :, None]
    selector = matches.astype(jnp.bfloat16)
    kept_mask = jnp.sum(matches.astype(jnp.int32), axis=2)
    spread_qkv = jnp.einsum(
        "wsj,wjc->wsc", selector, projected, preferred_element_type=jnp.float32
    ).astype(jnp.bfloat16)
    received, received_mask = (
        lax.all_to_all(
            spread_qkv.reshape(local_windows, win_count, per_device * 3 * group_width),
            "win",
            split_axis=1,
            concat_axis=0,
            tiled=True,
        ),
        lax.all_to_all(
            kept_mask.reshape(local_windows, win_count, per_device),
            "win",
            split_axis=1,
            concat_axis=0,
            tiled=True,
        ),
    )
    heads_all = received.reshape(all_windows, per_device, 3, head_local, head_dim)
    position_mask = received_mask.reshape(all_windows, per_device)
    mask_float = position_mask.astype(jnp.float32)
    key_mask = mask_float.T[:, None, None, :]
    query_kept = mask_float.T[:, None, :]
    scores = (
        jnp.einsum(
            "wphd,uphd->phwu",
            heads_all[:, :, 0],
            heads_all[:, :, 1],
            preferred_element_type=jnp.float32,
        )
        * score_scale
    )
    exponent = jnp.exp(scores) * key_mask
    denominator = jnp.sum(exponent, axis=-1) + 1.0 - query_kept
    attn_weights = (exponent / denominator[..., None]).astype(jnp.bfloat16)
    attended = jnp.einsum(
        "phwu,uphd->wphd", attn_weights, heads_all[:, :, 2], preferred_element_type=jnp.float32
    ).astype(jnp.bfloat16)
    flat_attended = attended.reshape(all_windows, per_device * group_width)
    group_term = jnp.dot(
        flat_attended.reshape(all_windows * per_device, group_width),
        w_out,
        preferred_element_type=jnp.float32,
    ).astype(jnp.bfloat16)
    returned = lax.all_to_all(
        group_term.reshape(all_windows, per_device * model_width),
        "win",
        split_axis=0,
        concat_axis=1,
        tiled=True,
    ).reshape(local_windows, POSITIONS, model_width)
    picked = jnp.einsum("wsj,wsd->wjd", selector, returned, preferred_element_type=jnp.float32)
    summed = lax.psum_scatter(
        picked.astype(jnp.bfloat16), "pos", scatter_dimension=1, tiled=True
    ).astype(jnp.float32)
    residual = lax.dynamic_slice_in_dim(tokens, lax.axis_index("pos") * kept_rows, kept_rows, 1)
    return (residual.astype(jnp.float32) + summed).astype(jnp.bfloat16)


def solution(mesh):
    in_specs = (P("win", None, None), P("win", None), P(), P(None, "pos", None), P("pos", None))
    out_specs = P("win", "pos", None)
    return jax.shard_map(local, mesh=mesh, in_specs=in_specs, out_specs=out_specs, check_vma=False)
```

profile of v0, /device:TPU:8, one launch (start us, length us, event | category | flops | bytes accessed | tf_op | source)
XLA Modules:
  0.0 554.7 jit_solution(9411796207060111082)
XLA Ops:
  6.5 1.0 convert_reduce_fusion.1
  7.6 0.1 reshape.58
  7.7 0.7 copy.28
  8.4 11.7 %all-to-all-start.1 = ((s32[8,32,8]{2,0,1:T(8,128)}), s32[8,32,8]{2,0,1:T(8,128)S(1)}, u32[]{:S(2)}, u32[]{:S(2)}) async-start(s32[8,32,8]{2,0,1:T(8,128)} %copy.28), calls=%async_computation.1 | async-start | bytes 262144 | tf_op jit(solution)/shard_map/all_to_all | solution.py:54
  20.1 3.4 convert_reduce_fusion
  23.5 0.6 copy-done.2
  24.2 1.5 fusion.2
  25.7 1.6 fusion.4
  27.4 5.3 convert_bitcast_fusion
  32.7 3.1 convolution_convert_fusion.2
  35.8 6.4 %copy.23 = bf16[8,256,960]{2,1,0:T(8,128)(2,1)} copy(bf16[8,256,960]{1,2,0:T(8,128)(2,1)} %convolution_convert_fusion.2) | data formatting | bytes 7864320 | tf_op jit(solution)/shard_map/convert_element_type | solution.py:45
  42.2 8.2 %reshape.56 = bf16[8,32,7680]{2,1,0:T(8,128)(2,1)} reshape(bf16[8,256,960]{2,1,0:T(8,128)(2,1)} %copy.23) | data formatting | bytes 7864320 | tf_op jit(solution)/shard_map/reshape | solution.py:48
  50.4 6.1 %copy.24 = bf16[8,32,7680]{2,0,1:T(8,128)(2,1)} copy(bf16[8,32,7680]{2,1,0:T(8,128)(2,1)} %reshape.56) | data formatting | bytes 7864320 | tf_op jit(solution)/shard_map/reshape | solution.py:48
  56.5 9.8 %all-to-all-start = ((bf16[8,32,7680]{2,0,1:T(8,128)(2,1)}), bf16[8,32,7680]{2,0,1:T(8,128)(2,1)}, u32[]{:S(2)}, u32[]{:S(2)}) async-start(bf16[8,32,7680]{2,0,1:T(8,128)(2,1)} %copy.24), calls=%async_computation | async-start | bytes 7864320 | tf_op jit(solution)/shard_map/all_to_all | solution.py:47
  66.5 87.7 %all-to-all-done = bf16[8,32,7680]{2,0,1:T(8,128)(2,1)} async-done(((bf16[8,32,7680]{2,0,1:T(8,128)(2,1)}), bf16[8,32,7680]{2,0,1:T(8,128)(2,1)}, u32[]{:S(2)}, u32[]{:S(2)}) %all-to-all-start) | async-done | bytes 3932192 | tf_op jit(solution)/shard_map/all_to_all | solution.py:47
  154.2 10.3 %reshape.57 = bf16[256,8,3,2,160]{4,3,2,1,0:T(2,128)(2,1)} reshape(bf16[32,8,1,7680]{3,1,0,2:T(8,128)(2,1)} %bitcast.3) | data formatting | bytes 7864320 | tf_op jit(solution)/shard_map/reshape | solution.py:62
  164.5 7.6 %fusion.18 = (bf16[256,8,1,2,160]{4,3,2,1,0:T(2,128)(2,1)}, bf16[256,8,1,2,160]{4,3,2,1,0:T(2,128)(2,1)}, bf16[256,8,1,2,160]{4,3,2,1,0:T(2,128)(2,1)}) fusion(bf16[256,8,3,2,160]{4,3,2,1,0:T(2,128)(2,1)} %reshape.57), kind=kLoop, calls=%fused_computation.33 | loop fusion | bytes 7864320 | tf_op jit(solution)/shard_map/slice | solution.py:80
  172.0 4.7 copy.37
  176.7 6.0 %copy.38 = bf16[256,8,1,2,160]{0,4,3,1,2:T(8,128)(2,1)} copy(bf16[256,8,1,2,160]{4,3,2,1,0:T(2,128)(2,1)} %get-tuple-element.7) | data formatting | bytes 2621440
  182.7 4.4 fusion.5
  187.1 4.7 copy.36
  191.7 4.4 fusion.10
  196.1 6.1 %copy.31 = bf16[256,8,2,160]{3,2,1,0:T(2,128)(2,1)} copy(bf16[256,8,2,160]{0,3,2,1:T(8,128)(2,1)} %fusion.10) | data formatting | bytes 2621440 | tf_op jit(solution)/shard_map/convert_element_type | solution.py:81
  202.2 4.9 reshape_reshape.3
  207.1 8.2 %convolution_convert_fusion = bf16[2048,2560]{1,0:T(8,128)(2,1)} fusion(bf16[2048,320]{1,0:T(8,128)(2,1)S(1)} %reshape_reshape.3, bf16[320,2560]{1,0:T(8,128)(2,1)S(1)} %copy-done), kind=kOutput, calls=%fused_computation.4 | convolution fusion | flops 3360686080 | bytes 13434880 | tf_op jit(solution)/shard_map/dot_general | solution.py:83
  215.3 14.8 %all_to_all.34 = bf16[32,8,20480]{2,1,0:T(8,128)(2,1)} reshape(bf16[2048,2560]{1,0:T(8,128)(2,1)} %convolution_convert_fusion) | data formatting | bytes 20971520 | tf_op jit(solution)/shard_map/all_to_all | solution.py:88
  230.1 237.3 %all_to_all.40 = bf16[32,8,20480]{2,1,0:T(8,128)(2,1)} all-to-all(bf16[32,8,20480]{2,1,0:T(8,128)(2,1)} %all_to_all.34), channel_id=1, replica_groups=mesh['win'=32,'pos'=8] {'win'}, dimensions={0} | all-to-all | bytes 20971520 | tf_op jit(solution)/shard_map/all_to_all | solution.py:88
  467.4 13.7 %copy.32 = bf16[8,32,20480]{2,1,0:T(8,128)(2,1)} copy(bf16[8,32,20480]{2,0,1:T(8,128)(2,1)} %bitcast.42) | data formatting | bytes 20971520 | tf_op jit(solution)/shard_map/all_to_all | solution.py:88
  481.1 14.8 %reshape.59 = bf16[8,256,2560]{2,1,0:T(8,128)(2,1)} reshape(bf16[8,32,20480]{2,1,0:T(8,128)(2,1)} %copy.32) | data formatting | bytes 20971520 | tf_op jit(solution)/shard_map/reshape | solution.py:94
  495.9 8.0 %convolution_convert_fusion.1 = bf16[8,128,2560]{2,1,0:T(8,128)(2,1)} fusion(bf16[8,256,2560]{2,1,0:T(8,128)(2,1)} %reshape.59, s32[8,128]{1,0:T(8,128)S(1)} %copy-done.3), kind=kOutput, calls=%fused_computation.8 | convolution fusion | flops 1345060864 | bytes 15732736 | tf_op jit(solution)/shard_map/wsj,wsd->wjd/dot_general | solution.py:95
  504.0 41.7 %reduce-scatter.2.cloned.1.call-done = bf16[8,16,2560]{2,1,0:T(8,128)(2,1)} async-done(((bf16[8,128,2560]{2,1,0:T(8,128)(2,1)}), bf16[8,16,2560]{2,1,0:T(8,128)(2,1)}) %reduce-scatter.2.cloned.1.call-update) | async-done | bytes 655376 | tf_op jit(solution)/shard_map/reduce_scatter | solution.py:96
  545.6 2.3 add_convert_fusion
  (22 shorter events, 0.2 us)
Async XLA Ops:
  6.5 200.5 %copy-start = (bf16[320,2560]{1,0:T(8,128)(2,1)S(1)}, bf16[320,2560]{1,0:T(8,128)(2,1)}, u32[]{:S(2)}) copy-start(bf16[320,2560]{1,0:T(8,128)(2,1)} %param.9) | copy-start | bytes 4915204
  8.4 48.1 %all-to-all-start.1 = ((s32[8,32,8]{2,0,1:T(8,128)}), s32[8,32,8]{2,0,1:T(8,128)S(1)}, u32[]{:S(2)}, u32[]{:S(2)}) async-start(s32[8,32,8]{2,0,1:T(8,128)} %copy.28), calls=%async_computation.1 | async-start | bytes 262144 | tf_op jit(solution)/shard_map/all_to_all | solution.py:54
  20.1 4.0 copy-start.2
  20.1 5.5 copy-start.4
  24.2 3.2 slice-start
  25.7 1.7 slice-start.1
  27.4 5.3 copy-start.3
  56.5 97.7 %all-to-all-start = ((bf16[8,32,7680]{2,0,1:T(8,128)(2,1)}), bf16[8,32,7680]{2,0,1:T(8,128)(2,1)}, u32[]{:S(2)}, u32[]{:S(2)}) async-start(bf16[8,32,7680]{2,0,1:T(8,128)(2,1)} %copy.24), calls=%async_computation | async-start | bytes 7864320 | tf_op jit(solution)/shard_map/all_to_all | solution.py:47
  66.4 479.2 %reduce-scatter.2.cloned.1.call-start = ((), (), s32[]{:S(2)}) async-start(), calls=%async_computation.4 | async-start | bytes 5898240 | tf_op jit(solution)/shard_map/reduce_scatter | solution.py:96
  495.9 52.0 %copy-start.1 = (bf16[320,2560]{1,0:T(8,128)(2,1)S(1)}, bf16[320,2560]{1,0:T(8,128)(2,1)}, u32[]{:S(2)}) copy-start(bf16[320,2560]{1,0:T(8,128)(2,1)} %param.9) | copy-start | bytes 4915204
Sparse Core Ops, SparseCore 0:
  504.1 41.4 reduce-scatter.1
where the time goes:
time: 557 us; the launch traced here: 555 us
  blocking collectives  237 us (43%)
  waiting for transfers between devices  129 us (23%)
  local copies, waits for them, and re-layouts  110 us (20%)
  matrix products  33.4 us (6%)
  starting transfers between devices  21.6 us (4%)
  between operations  13.6 us (2%)
  other arithmetic  9.84 us (2%)
    all_to_all x1, blocking collectives, local(): lax.all_to_all(group_term.reshape(all_windows, per_device * model_width),...  237 us
    all_to_all x1, waiting for transfers between devices, local(): lax.all_to_all(spread_qkv.reshape(local_windows, win_count, per_device *...  87.7 us
    reduce_scatter x1, waiting for transfers between devices, local(): lax.psum_scatter(picked.astype(jnp.bfloat16), 'pos', scatter_dimension=1,...  41.7 us
    all_to_all x2, local copies, waits for them, and re-layouts, local(): lax.all_to_all(group_term.reshape(all_windows, per_device * model_width),...  28.5 us
    unnamed x17, local copies, waits for them, and re-layouts  15.9 us
    reshape x1, local copies, waits for them, and re-layouts, local(): returned = lax.all_to_all(group_term.reshape(all_windows, per_device * mo...  14.8 us
    reshape x2, local copies, waits for them, and re-layouts, local(): spread_qkv.reshape(local_windows, win_count, per_device * 3 * group_width)  14.3 us
    all_to_all x1, starting transfers between devices, local(): lax.all_to_all(kept_mask.reshape(local_windows, win_count, per_device), '...  11.7 us
  transfers between devices with their start and end apart: 3, of which 2 were waited for; matrix products, arithmetic and copies ran while one was open for 6% of the time, Pallas kernels for 0%

commit v1 on v0

v1 whole, which is shorter than its diff:
```python
import math

import jax
import jax.numpy as jnp
from jax import lax
from jax.experimental import pallas as pl
from jax.experimental.pallas import tpu as pltpu
from jax.sharding import PartitionSpec as P

D = 2560
HEADS = 16
HEAD_DIM = D // HEADS
POSITIONS = 256
PAIRS = POSITIONS // 2
NORM_EPSILON = 1e-05
SLOT = 512
FLAG = 3 * HEAD_DIM

F32 = jnp.float32
BF16 = jnp.bfloat16


def project_kernel(tokens_ref, keep_ref, gain_ref, w_hbm, out_ref, w_ref, rows_ref, sems):
    step = pl.program_id(0)
    windows, pairs, _ = tokens_ref.shape
    rows = windows * pairs

    def copies():
        made = []
        for head in range(2):
            for c in range(3):
                made.append(pltpu.make_async_copy(
                    w_hbm.at[c, pl.ds(head * HEAD_DIM, HEAD_DIM)],
                    w_ref.at[pl.ds(head * SLOT + c * HEAD_DIM, HEAD_DIM)],
                    sems.at[head * 3 + c],
                ))
        return made

    @pl.when(step == 0)
    def _():
        for copy in copies():
            copy.start()
        for head in range(2):
            w_ref[head * SLOT + FLAG:(head + 1) * SLOT, :] = jnp.zeros((SLOT - FLAG, D), BF16)

    for w in range(windows):
        x = tokens_ref[w].astype(F32)
        mean = jnp.sum(x, axis=-1, keepdims=True) * (1.0 / D)
        centered = x - mean
        variance = jnp.sum(centered * centered, axis=-1, keepdims=True) * (1.0 / D)
        normed = centered * lax.rsqrt(variance + NORM_EPSILON) * gain_ref[...]
        for c in range(D // 128):
            rows_ref[c, pl.ds(w, pairs, stride=windows), :] = normed[:, c * 128:(c + 1) * 128]

    @pl.when(step == 0)
    def _():
        for copy in copies():
            copy.wait()

    projected = lax.dot_general(
        jnp.concatenate([rows_ref[c].astype(BF16) for c in range(D // 128)], axis=-1),
        w_ref[...],
        (((1,), (1,)), ((), ())),
        preferred_element_type=F32,
    )
    parity = (keep_ref[...] & 1).astype(F32)
    row = lax.broadcasted_iota(jnp.int32, (rows, windows), 0)
    pick_window = (row % windows == lax.broadcasted_iota(jnp.int32, (rows, windows), 1)).astype(F32)
    spread = jnp.dot(pick_window, parity, preferred_element_type=F32)
    row_pair = lax.broadcasted_iota(jnp.int32, spread.shape, 0) // windows + step * pairs
    mine = row_pair == lax.broadcasted_iota(jnp.int32, spread.shape, 1)
    odd = jnp.sum(jnp.where(mine, spread, 0.0), axis=-1, keepdims=True)
    tail_lane = lax.broadcasted_iota(jnp.int32, (rows, 128), 1)
    first_flag = FLAG - (SLOT - 128)
    for head in range(2):
        part = projected[:, head * SLOT:(head + 1) * SLOT]
        tail = part[:, SLOT - 128:]
        tail = jnp.where(tail_lane == first_flag, odd, jnp.where(tail_lane == first_flag + 1, 1.0 - odd, tail))
        blocks = pairs // 16
        for b in range(blocks):
            lo, hi = b * 16 * windows, (b + 1) * 16 * windows
            out_ref[head, :, b, :, :SLOT - 128] = (
                part[lo:hi, :SLOT - 128].reshape(16, windows, SLOT - 128).astype(BF16)
            )
            out_ref[head, :, b, :, SLOT - 128:] = tail[lo:hi].reshape(16, windows, 128).astype(BF16)


def project(tokens, keep_index, norm_gain, w_qkv):
    windows, keep, _ = tokens.shape
    pos_count = 8
    blocks_per_step = 2
    pairs = 16 * blocks_per_step
    return pl.pallas_call(
        project_kernel,
        grid=(keep // pairs,),
        in_specs=[
            pl.BlockSpec((windows, pairs, D), lambda s: (0, s, 0)),
            pl.BlockSpec((windows, keep), lambda s: (0, 0)),
            pl.BlockSpec((1, D), lambda s: (0, 0)),
            pl.BlockSpec(memory_space=pl.ANY),
        ],
        out_specs=pl.BlockSpec((2, 16, blocks_per_step, windows, SLOT), lambda s: (0, 0, s, 0, 0)),
        out_shape=jax.ShapeDtypeStruct((2, 16, pos_count, windows, SLOT), BF16),
        scratch_shapes=[
            pltpu.VMEM((2 * SLOT, D), BF16),
            pltpu.VMEM((D // 128, windows * pairs, 128), F32),
            pltpu.SemaphoreType.DMA((6,)),
        ],
        compiler_params=pltpu.CompilerParams(vmem_limit_bytes=48 * 1024 * 1024),
        cost_estimate=pl.CostEstimate(flops=2 * 1024 * 1024 * D, bytes_accessed=14_000_000, transcendentals=0),
    )(tokens, keep_index, norm_gain.reshape(1, D), w_qkv)


def attend_kernel(in_ref, out_ref):
    senders, groups, windows, _ = in_ref.shape
    total = senders * windows
    scale = 1.0 / math.sqrt(HEAD_DIM)
    flags = in_ref[:, 0, :, SLOT - 128:].astype(F32).reshape(total, 128)
    lane = lax.broadcasted_iota(jnp.int32, flags.shape, 1)
    flags = jnp.where(lane >= FLAG - (SLOT - 128), flags, 0.0).astype(BF16)
    same = lax.dot_general(flags, flags, (((1,), (1,)), ((), ())), preferred_element_type=F32) > 0.5
    results = []
    for g in range(groups):
        block = in_ref[:, g].astype(F32).reshape(total, SLOT).astype(BF16)
        query = block[:, :HEAD_DIM]
        key = block[:, HEAD_DIM:2 * HEAD_DIM]
        value = block[:, 2 * HEAD_DIM:3 * HEAD_DIM]
        scores = lax.dot_general(query, key, (((1,), (1,)), ((), ())), preferred_element_type=F32) * scale
        scores = jnp.where(same, scores, -jnp.inf)
        top = jnp.max(scores, axis=-1, keepdims=True)
        exponent = jnp.exp(scores - top)
        weights = exponent * (1.0 / jnp.sum(exponent, axis=-1, keepdims=True))
        results.append(jnp.dot(weights.astype(BF16), value, preferred_element_type=F32))
    attended = jnp.concatenate(results, axis=-1)
    out_ref[...] = attended.reshape(senders, windows, groups * HEAD_DIM).astype(BF16)


def attend(received):
    senders, groups, windows, _ = received.shape
    return pl.pallas_call(
        attend_kernel,
        out_shape=jax.ShapeDtypeStruct((senders, windows, groups * HEAD_DIM), BF16),
        compiler_params=pltpu.CompilerParams(vmem_limit_bytes=48 * 1024 * 1024),
        cost_estimate=pl.CostEstimate(flops=8 * 4 * 256 ** 3, bytes_accessed=2_800_000, transcendentals=8 * 65536),
    )(received)


def finish_kernel(place_ref, attended_ref, w_ref, tokens_ref, out_ref, sum_ref):
    windows = attended_ref.shape[2]
    pairs = attended_ref.shape[1]
    columns = out_ref.shape[2]
    depth = attended_ref.shape[3]
    total = None
    for head in range(2):
        rows = attended_ref[head].astype(F32).reshape(pairs * windows, depth).astype(BF16)
        term = jnp.dot(rows, w_ref[:, head].reshape(depth, columns), preferred_element_type=F32)
        total = term if total is None else total + term
    for c in range(columns // 128):
        sum_ref[c] = total[:, c * 128:(c + 1) * 128]
    for w in range(windows):
        for c in range(columns // 128):
            lanes = slice(c * 128, (c + 1) * 128)
            added = sum_ref[c, pl.ds(w, pairs, stride=windows), :]
            out_ref[w, :, lanes] = (tokens_ref[w, :, lanes].astype(F32) + added).astype(BF16)


def finish(place, attended, w_all, tokens):
    windows = tokens.shape[0]
    columns = 512
    return pl.pallas_call(
        finish_kernel,
        grid_spec=pltpu.PrefetchScalarGridSpec(
            num_scalar_prefetch=1,
            grid=(D // columns,),
            in_specs=[
                pl.BlockSpec((2, 16, windows, 8 * HEAD_DIM), lambda n, place: (0, 0, 0, 0)),
                pl.BlockSpec((8, 2, HEAD_DIM, columns), lambda n, place: (0, 0, 0, n)),
                pl.BlockSpec((windows, 16, columns), lambda n, place: (0, place[0], n)),
            ],
            out_specs=pl.BlockSpec((windows, 16, columns), lambda n, place: (0, 0, n)),
            scratch_shapes=[pltpu.VMEM((columns // 128, windows * 16, 128), F32)],
        ),
        out_shape=jax.ShapeDtypeStruct((windows, 16, D), BF16),
        compiler_params=pltpu.CompilerParams(vmem_limit_bytes=48 * 1024 * 1024),
        cost_estimate=pl.CostEstimate(flops=2 * 128 * D * D, bytes_accessed=15_000_000, transcendentals=0),
    )(place, attended, w_all, tokens)


def local(tokens, keep_index, norm_gain, w_qkv, w_out):
    windows = tokens.shape[0]
    w_all = lax.all_gather(w_out, "pos", axis=0, tiled=False)
    sent = project(tokens, keep_index, norm_gain, w_qkv)
    received = lax.all_to_all(
        sent.reshape(256, windows, SLOT), ("win", "pos"), split_axis=0, concat_axis=0, tiled=True
    )
    attended = attend(received.reshape(32, 8, windows, SLOT))
    returned = lax.all_to_all(attended, "win", split_axis=0, concat_axis=0, tiled=True)
    place = lax.axis_index("pos").astype(jnp.int32).reshape(1)
    return finish(
        place,
        returned.reshape(2, 16, windows, 8 * HEAD_DIM),
        w_all.reshape(8, 2, HEAD_DIM, D),
        tokens,
    )


def solution(mesh):
    in_specs = (P("win", None, None), P("win", None), P(), P(None, "pos", None), P("pos", None))
    out_specs = P("win", "pos", None)
    return jax.shard_map(local, mesh=mesh, in_specs=in_specs, out_specs=out_specs, check_vma=False)
```

time: 557 us -> 138 us (0.25)
  blocking collectives: 237 us -> 66.8 us
  waiting for transfers between devices: 129 us -> 18.2 us
  local copies, waits for them, and re-layouts: 110 us -> 3.89 us
  matrix products: 33.4 us -> 0 us
  Pallas kernels: 0 us -> 26.8 us
  starting transfers between devices: 21.6 us -> 6.33 us
  other arithmetic: 9.84 us -> 0 us
    all_to_all x1, blocking collectives: 237 us -> 66.8 us  [local(): lax.all_to_all(sent.reshape(256, windows, SLOT), ('win', 'pos'), split_ax...]
    all_to_all x2 -> x1, waiting for transfers between devices: 87.7 us -> 17.5 us  [local(): lax.all_to_all(attended, 'win', split_axis=0, concat_axis=0, tiled=True)]
    reduce_scatter x1 -> x0, waiting for transfers between devices: 41.7 us -> none  [local(): lax.psum_scatter(picked.astype(jnp.bfloat16), 'pos', scatter_dimension=1,...]
    reshape x6 -> x1, local copies, waits for them, and re-layouts: 40.2 us -> 0.72 us  [project(): norm_gain.reshape(1, D)]
    dot_general x6 -> x0, matrix products: 33.4 us -> none  [the longest x1 8.24 us: local(): jnp.dot(flat_attended.reshape(all_windows * per_device, group_width), w_o...]
    all_to_all x2 -> x0, local copies, waits for them, and re-layouts: 28.5 us -> none  [local(): lax.all_to_all(group_term.reshape(all_windows, per_device * model_width),...]
    pallas_call x0 -> x3, Pallas kernels: none -> 26.8 us  [the longest x1 14.8 us: project(): pl.pallas_call(project_kernel, grid=(keep // pairs,), in_specs=[pl.BlockS...]
    all_to_all x2 -> x1, starting transfers between devices: 21.5 us -> 6.33 us  [local(): lax.all_to_all(attended, 'win', split_axis=0, concat_axis=0, tiled=True)]
  transfers between devices with their start and end apart: 3 -> 2, of which waited for: 2 -> 1; matrix products, arithmetic and copies ran while one was open for 6% -> 1% of each run, Pallas kernels for 0% -> 14%
where the time goes in v1:
time: 138 us; the launch traced here: 135 us
  blocking collectives  66.8 us (48%)
  Pallas kernels  26.8 us (19%)
  waiting for transfers between devices  18.2 us (13%)
  between operations  13.4 us (10%)
  starting transfers between devices  6.33 us (5%)
  local copies, waits for them, and re-layouts  3.89 us (3%)
    all_to_all x1, blocking collectives, local(): lax.all_to_all(sent.reshape(256, windows, SLOT), ('win', 'pos'), split_ax...  66.8 us
    all_to_all x1, waiting for transfers between devices, local(): lax.all_to_all(attended, 'win', split_axis=0, concat_axis=0, tiled=True)  17.5 us
    pallas_call x1, Pallas kernels, project(): pl.pallas_call(project_kernel, grid=(keep // pairs,), in_specs=[pl.BlockS...  14.8 us
    pallas_call x1, Pallas kernels, finish(): pl.pallas_call(finish_kernel, grid_spec=pltpu.PrefetchScalarGridSpec(num_...  7.86 us
    all_to_all x1, starting transfers between devices, local(): lax.all_to_all(attended, 'win', split_axis=0, concat_axis=0, tiled=True)  6.33 us
    pallas_call x1, Pallas kernels, attend(): pl.pallas_call(attend_kernel, out_shape=jax.ShapeDtypeStruct((senders, wi...  4.14 us
    unnamed x4, local copies, waits for them, and re-layouts  3.17 us
  transfers between devices with their start and end apart: 2, of which 1 were waited for; matrix products, arithmetic and copies ran while one was open for 1% of the time, Pallas kernels for 14%

profile of v1, /device:TPU:8, one launch (start us, length us, event | category | flops | bytes accessed | tf_op | source)
XLA Modules:
  0.0 135.4 jit_solution(137192295673789280)
XLA Ops:
  6.5 0.0 all-gather.3.cloned.1.call-start
  6.5 0.7 all-gather.3.cloned.1.call-update
  7.3 0.7 reshape.19.gain_ref
  8.0 0.0 copy-start.1
  8.0 0.7 copy-done.1
  8.7 14.8 %shard_map.55 = bf16[2,16,8,8,512]{4,3,2,1,0:T(8,128)(2,1)S(1)} custom-call(bf16[8,128,2560]{2,1,0:T(8,128)(2,1)} %tokens_ref.3, s32[8,128]{1,0:T(8,128)S(1)} %copy-done.1, f32[1,2560]{1,0:T(1,128)S(1)} %reshape.19.gain_ref, bf16[3,320,2560]{2,1,0:T(8,128)(2,1)} %w_hbm.1), custom_call_target="tpu_custom_call" | custom-call | flops 5368709120 | bytes 14000000 | tf_op jit(solution)/shard_map/pallas_call | solution.py:93
  23.4 66.8 %all_to_all.10 = bf16[256,8,512]{2,1,0:T(8,128)(2,1)S(1)} all-to-all(bf16[256,8,512]{2,1,0:T(8,128)(2,1)S(1)} %bitcast.7), channel_id=1, replica_groups=mesh['win'=32,'pos'=8] {'win','pos'}, dimensions={0} | all-to-all | bytes 4194304 | tf_op jit(solution)/shard_map/all_to_all | solution.py:193
  90.2 4.1 %shard_map.56 = bf16[32,8,1280]{2,1,0:T(8,128)(2,1)} custom-call(bf16[32,8,8,512]{3,2,1,0:T(8,128)(2,1)S(1)} %bitcast.5), custom_call_target="tpu_custom_call" | custom-call | flops 536870912 | bytes 2800000 | tf_op jit(solution)/shard_map/pallas_call | solution.py:140
  94.4 6.3 %all-to-all-start.1 = ((bf16[32,8,1280]{2,1,0:T(8,128)(2,1)}), bf16[32,8,1280]{2,1,0:T(8,128)(2,1)S(1)}, u32[]{:S(2)}, u32[]{:S(2)}) async-start(bf16[32,8,1280]{2,1,0:T(8,128)(2,1)} %shard_map.56), calls=%async_computation.1 | async-start | bytes 1310720 | tf_op jit(solution)/shard_map/all_to_all | solution.py:197
  100.7 17.5 %all-to-all-done.1 = bf16[32,8,1280]{2,1,0:T(8,128)(2,1)S(1)} async-done(((bf16[32,8,1280]{2,1,0:T(8,128)(2,1)}), bf16[32,8,1280]{2,1,0:T(8,128)(2,1)S(1)}, u32[]{:S(2)}, u32[]{:S(2)}) %all-to-all-start.1) | async-done | bytes 655392 | tf_op jit(solution)/shard_map/all_to_all | solution.py:197
  118.2 0.0 all-gather.3.cloned.1.call-done
  118.2 0.0 copy-start
  118.2 2.5 %copy-done = bf16[8,128,2560]{2,1,0:T(8,128)(2,1)S(1)} copy-done((bf16[8,128,2560]{2,1,0:T(8,128)(2,1)S(1)}, bf16[8,128,2560]{2,1,0:T(8,128)(2,1)}, u32[]{:S(2)}) %copy-start) | copy-done | bytes 5242904
  120.7 7.9 %shard_map.57 = bf16[8,16,2560]{2,1,0:T(8,128)(2,1)} custom-call(s32[1]{0:T(128)} %bitcast.place_ref, bf16[2,16,8,1280]{3,2,1,0:T(8,128)(2,1)S(1)} %bitcast.6, bf16[8,2,160,2560]{3,2,1,0:T(8,128)(2,1)} %bitcast.8, bf16[8,128,2560]{2,1,0:T(8,128)(2,1)S(1)} %copy-done), custom_call_target="tpu_custom_call" | custom-call | flops 1677721600 | bytes 15000000 | tf_op jit(solution)/shard_map/pallas_call | solution.py:170
Async XLA Ops:
  6.5 111.7 %all-gather.3.cloned.1.call-start = ((), (), s32[]{:S(2)}) async-start(), calls=%async_computation.2 | async-start | bytes 14745600 | tf_op jit(solution)/shard_map/all_gather | solution.py:191
  8.0 0.7 copy-start.1
  94.4 23.8 %all-to-all-start.1 = ((bf16[32,8,1280]{2,1,0:T(8,128)(2,1)}), bf16[32,8,1280]{2,1,0:T(8,128)(2,1)S(1)}, u32[]{:S(2)}, u32[]{:S(2)}) async-start(bf16[32,8,1280]{2,1,0:T(8,128)(2,1)} %shard_map.56), calls=%async_computation.1 | async-start | bytes 1310720 | tf_op jit(solution)/shard_map/all_to_all | solution.py:197
  118.2 2.5 %copy-start = (bf16[8,128,2560]{2,1,0:T(8,128)(2,1)S(1)}, bf16[8,128,2560]{2,1,0:T(8,128)(2,1)}, u32[]{:S(2)}) copy-start(bf16[8,128,2560]{2,1,0:T(8,128)(2,1)} %tokens_ref.3) | copy-start | bytes 15728644
Sparse Core Ops, SparseCore 0:
  9.2 97.3 all-gather.2

commit v2 on v0

v2 whole, which is shorter than its diff:
```python
import math

import jax
import jax.numpy as jnp
from jax import lax
from jax.experimental import pallas as pl
from jax.experimental.pallas import tpu as pltpu
from jax.sharding import Mesh, PartitionSpec as P

D = 2560
HEADS = 16
HEAD_DIM = D // HEADS
GROUP = 2 * HEAD_DIM
NORM_EPSILON = 1e-05
WINDOWS = 8
PAIRS = 128
SLOT = 512
FLAG = 3 * HEAD_DIM
LAST = SLOT - 128
X_COUNT = 4
PLANE = 32

F32 = jnp.float32
BF16 = jnp.bfloat16
VMEM = pl.BlockSpec(memory_space=pltpu.VMEM)
HBM = pl.BlockSpec(memory_space=pltpu.HBM)
LIMIT = 60 * 1024 * 1024

BLOCK = 32
BLOCKS = PAIRS // BLOCK


def project_kernel(tokens_hbm, keep_hbm, gain_hbm, w_hbm, out_hbm, out_ref, gain_ref, x_ref, keep_ref, w_ref, spread_ref, *rest):
    rows_refs, sems = rest[:BLOCKS], rest[BLOCKS]
    rows = WINDOWS * BLOCK
    token_copies = [
        pltpu.make_async_copy(tokens_hbm.at[:, pl.ds(b * BLOCK, BLOCK)], x_ref.at[b], sems.at[b, 0])
        for b in range(BLOCKS)
    ]
    w_copies = [
        [
            pltpu.make_async_copy(
                w_hbm.at[c, pl.ds(h * HEAD_DIM, HEAD_DIM)],
                w_ref.at[pl.ds(h * SLOT + c * HEAD_DIM, HEAD_DIM)],
                sems.at[BLOCKS + h, c],
            )
            for c in range(3)
        ]
        for h in range(2)
    ]
    keep_copy = pltpu.make_async_copy(keep_hbm, keep_ref, sems.at[BLOCKS + 2, 0])
    gain_copy = pltpu.make_async_copy(gain_hbm, gain_ref, sems.at[BLOCKS + 2, 1])
    out_copies = [
        pltpu.make_async_copy(
            out_ref.at[pl.ds(b * BLOCK, BLOCK)], out_hbm.at[pl.ds(b * BLOCK, BLOCK)], sems.at[BLOCKS + 2, 2 + b]
        )
        for b in range(BLOCKS)
    ]
    gain_copy.start()
    for copy in [token_copies[0]] + w_copies[0]:
        copy.start()
    keep_copy.start()
    for h in range(2):
        w_ref[h * SLOT + FLAG:(h + 1) * SLOT, :] = jnp.zeros((SLOT - FLAG, D), BF16)
    gain_copy.wait()
    gain = gain_ref[...].reshape(1, D)

    def norm(b, w):
        x = x_ref[b, w].astype(F32)
        mean = jnp.sum(x, axis=-1, keepdims=True) * (1.0 / D)
        centered = x - mean
        variance = jnp.sum(centered * centered, axis=-1, keepdims=True) * (1.0 / D)
        normed = centered * lax.rsqrt(variance + NORM_EPSILON) * gain
        rows_refs[b][w * BLOCK:(w + 1) * BLOCK, :] = normed.astype(BF16)

    row = lax.broadcasted_iota(jnp.int32, (rows, WINDOWS), 0)
    pick_window = (row // BLOCK == lax.broadcasted_iota(jnp.int32, (rows, WINDOWS), 1)).astype(F32)
    lane = lax.broadcasted_iota(jnp.int32, (rows, 128), 1)
    row_pair = lax.broadcasted_iota(jnp.int32, (rows, 128), 0) % BLOCK

    token_copies[0].wait()
    for copy in w_copies[1] + [token_copies[1]]:
        copy.start()
    for w in range(WINDOWS):
        norm(0, w)
    keep_copy.wait()
    spread = jnp.dot(pick_window, (keep_ref[...] & 1).astype(F32), preferred_element_type=F32)
    for b in range(BLOCKS):
        if b + 2 < BLOCKS:
            token_copies[b + 2].start()
        odd = jnp.sum(jnp.where(row_pair + b * BLOCK == lane, spread, 0.0), axis=-1, keepdims=True)
        for h in range(2):
            if b == 0:
                for copy in w_copies[h]:
                    copy.wait()
            part = lax.dot_general(
                rows_refs[b][...],
                w_ref[h * SLOT:(h + 1) * SLOT, :],
                (((1,), (1,)), ((), ())),
                preferred_element_type=F32,
            )
            for c in range(SLOT // 128):
                lanes = slice(c * 128, (c + 1) * 128)
                piece = part[:, lanes]
                if c == LAST // 128:
                    piece = jnp.where(
                        lane == FLAG - LAST, odd, jnp.where(lane == FLAG - LAST + 1, 1.0 - odd, piece)
                    )
                at = h * (SLOT // 128) + c
                for w in range(WINDOWS):
                    spread_ref[b % 2, at, pl.ds(w, BLOCK, stride=WINDOWS), :] = piece[w * BLOCK:(w + 1) * BLOCK]
                out_ref[b * BLOCK:(b + 1) * BLOCK, h, :, lanes] = (
                    spread_ref[b % 2, at].reshape(BLOCK, WINDOWS, 128).astype(BF16)
                )
        out_copies[b].start()
        if b + 1 < BLOCKS:
            token_copies[b + 1].wait()
            for w in range(WINDOWS):
                norm(b + 1, w)
    for copy in out_copies:
        copy.wait()


def project(tokens, keep_index, norm_gain, w_qkv):
    rows = WINDOWS * BLOCK
    return pl.pallas_call(
        project_kernel,
        in_specs=[HBM, HBM, HBM, HBM],
        out_specs=HBM,
        out_shape=jax.ShapeDtypeStruct((PAIRS, 2, WINDOWS, SLOT), BF16),
        scratch_shapes=[
            pltpu.VMEM((PAIRS, 2, WINDOWS, SLOT), BF16),
            pltpu.VMEM((D,), F32),
            pltpu.VMEM((BLOCKS, WINDOWS, BLOCK, D), BF16),
            pltpu.VMEM((WINDOWS, PAIRS), jnp.int32),
            pltpu.VMEM((2 * SLOT, D), BF16),
            pltpu.VMEM((2, 2 * SLOT // 128, rows, 128), F32),
        ]
        + [pltpu.VMEM((rows, D), BF16)] * BLOCKS
        + [pltpu.SemaphoreType.DMA((BLOCKS + 3, WINDOWS))],
        compiler_params=pltpu.CompilerParams(vmem_limit_bytes=LIMIT),
        cost_estimate=pl.CostEstimate(flops=2 * 1024 * 1024 * D, bytes_accessed=14_000_000, transcendentals=0),
    )(tokens, keep_index, norm_gain, w_qkv)


def attend_kernel(in_ref, out_ref):
    total = PLANE * WINDOWS
    scale = 1.0 / math.sqrt(HEAD_DIM)
    flags = in_ref[0, :, 0, :, LAST:].astype(F32).reshape(total, 128)
    lane = lax.broadcasted_iota(jnp.int32, flags.shape, 1)
    flags = jnp.where(lane >= FLAG - LAST, flags, 0.0).astype(BF16)
    same = lax.dot_general(flags, flags, (((1,), (1,)), ((), ())), preferred_element_type=F32) > 0.5
    me = lax.axis_index("x")
    heads, tails = [], []
    for d in range(X_COUNT):
        source = lax.rem(me - d + X_COUNT, X_COUNT)
        group = []
        for h in range(2):
            block = in_ref[source, :, h].astype(F32).reshape(total, SLOT).astype(BF16)
            query = block[:, :HEAD_DIM]
            key = block[:, HEAD_DIM:2 * HEAD_DIM]
            value = block[:, 2 * HEAD_DIM:3 * HEAD_DIM]
            scores = lax.dot_general(query, key, (((1,), (1,)), ((), ())), preferred_element_type=F32) * scale
            scores = jnp.where(same, scores, -jnp.inf)
            top = jnp.max(scores, axis=-1, keepdims=True)
            exponent = jnp.exp(scores - top)
            weights = exponent * (1.0 / jnp.sum(exponent, axis=-1, keepdims=True))
            group.append(jnp.dot(weights.astype(BF16), value, preferred_element_type=F32))
        group = jnp.concatenate(group, axis=-1)
        heads.append(group[:, :256])
        tails.append(group[:, 256:])
    attended = jnp.concatenate(heads + tails, axis=-1)
    out_ref[...] = attended.reshape(PLANE, WINDOWS, X_COUNT * GROUP).astype(BF16)


def attend(received):
    return pl.pallas_call(
        attend_kernel,
        in_specs=[VMEM],
        out_specs=VMEM,
        out_shape=jax.ShapeDtypeStruct((PLANE, WINDOWS, X_COUNT * GROUP), BF16),
        compiler_params=pltpu.CompilerParams(vmem_limit_bytes=48 * 1024 * 1024),
        cost_estimate=pl.CostEstimate(flops=8 * 4 * 256 ** 3, bytes_accessed=2_800_000, transcendentals=8 * 65536),
    )(received)


CHUNK = 512
CHUNKS = D // CHUNK


def finish_kernel(attended_ref, w0, w1, w2a, w2b, w3, tokens_hbm, own_ref, other_ref, w_ref, t_ref, x_ref, rows_ref, sems):
    core = lax.axis_index("c")
    first = pl.multiple_of((lax.axis_index("x") * 2 + core) * 16, 16)
    token_copy = pltpu.make_async_copy(tokens_hbm.at[:, pl.ds(first, 16)], t_ref, sems.at[CHUNKS, 0])
    parts = []
    for d, w in ((0, w0), (1, w1), (3, w3)):
        parts += [(w, 0, 256, d * 256), (w, 256, 64, 1024 + d * 64)]
    parts += [(w2a, 0, 160, 512), (w2b, 0, 96, 672), (w2b, 96, 64, 1152)]
    copies = [
        [
            pltpu.make_async_copy(
                w.at[pl.ds(lo, size), pl.ds(n * CHUNK, CHUNK)],
                w_ref.at[pl.ds(to, size), pl.ds(n * CHUNK, CHUNK)],
                sems.at[n, i],
            )
            for i, (w, lo, size, to) in enumerate(parts)
        ]
        for n in range(CHUNKS)
    ]
    for copy in copies[0]:
        copy.start()
    token_copy.start()
    for n in range(1, CHUNKS):
        for copy in copies[n]:
            copy.start()
    for c in range(X_COUNT * GROUP // 128):
        lanes = slice(c * 128, (c + 1) * 128)
        x_ref[c] = attended_ref[:, :, lanes].astype(F32).reshape(PLANE * WINDOWS, 128)
        for half, start in ((0, core * 128), (1, (1 - core) * 128)):
            for w in range(WINDOWS):
                to = half * 128 + w * 16
                rows_ref[to:to + 16, lanes] = x_ref[c, pl.ds(start + w, 16, stride=WINDOWS), :].astype(BF16)
    for n in range(CHUNKS):
        lanes = slice(n * CHUNK, (n + 1) * CHUNK)
        for copy in copies[n]:
            copy.wait()
        total = jnp.dot(rows_ref[...], w_ref[:, lanes], preferred_element_type=F32)
        if n == 0:
            token_copy.wait()
        own_ref[:, :, lanes] = t_ref[:, :, lanes].astype(F32) + total[:128].reshape(WINDOWS, 16, CHUNK)
        other_ref[:, :, lanes] = total[128:].reshape(WINDOWS, 16, CHUNK).astype(BF16)


def finish(attended, weights, tokens):
    return pl.pallas_call(
        finish_kernel,
        in_specs=[VMEM] + [HBM] * 6,
        out_specs=(VMEM, VMEM),
        out_shape=(
            jax.ShapeDtypeStruct((WINDOWS, 16, D), F32),
            jax.ShapeDtypeStruct((WINDOWS, 16, D), BF16),
        ),
        scratch_shapes=[
            pltpu.VMEM((X_COUNT * GROUP, D), BF16),
            pltpu.VMEM((WINDOWS, 16, D), BF16),
            pltpu.VMEM((X_COUNT * GROUP // 128, PLANE * WINDOWS, 128), F32),
            pltpu.VMEM((PLANE * WINDOWS, X_COUNT * GROUP), BF16),
            pltpu.SemaphoreType.DMA((CHUNKS + 1, 9)),
        ],
        compiler_params=pltpu.CompilerParams(vmem_limit_bytes=50 * 1024 * 1024),
        cost_estimate=pl.CostEstimate(flops=2 * 256 * 1280 * D, bytes_accessed=9_000_000, transcendentals=0),
    )(attended, *weights, tokens)


def shift(value, axis, by):
    count = lax.axis_size(axis)
    return lax.ppermute(value, axis, [(i, (i + by) % count) for i in range(count)])


def local(tokens, keep_index, norm_gain, w_qkv, w_out):
    w1 = shift(w_out, "x", 1)
    w3 = shift(w_out, "x", -1)
    w2a = shift(w1[:HEAD_DIM], "x", 1)
    w2b = shift(w3[HEAD_DIM:], "x", -1)
    sent = project(tokens, keep_index, norm_gain, w_qkv)
    received = lax.all_to_all(
        sent.reshape(X_COUNT * PLANE, 2 * WINDOWS, SLOT), ("x", "y", "z"), split_axis=0, concat_axis=0, tiled=True
    )
    attended = attend(received.reshape(X_COUNT, PLANE, 2, WINDOWS, SLOT))
    returned = lax.all_to_all(attended, ("y", "z"), split_axis=0, concat_axis=0, tiled=True)
    own, other = finish(returned, (w_out, w1, w2a, w2b, w3), tokens)
    return (own + shift(other, "c", 1).astype(F32)).astype(BF16)


def solution(mesh):
    mesh = Mesh(mesh.devices.reshape(4, 8, 4, 2), ("y", "z", "x", "c"))
    win, pos = ("y", "z"), ("x", "c")
    in_specs = (P(win, None, None), P(win, None), P(), P(None, pos, None), P(pos, None))
    return jax.shard_map(local, mesh=mesh, in_specs=in_specs, out_specs=P(win, pos, None), check_vma=False)
```

time: 557 us -> 124 us (0.22)
  blocking collectives: 237 us -> 0 us
  local copies, waits for them, and re-layouts: 110 us -> 2.4 us
  waiting for transfers between devices: 129 us -> 64.8 us
  matrix products: 33.4 us -> 0 us
  Pallas kernels: 0 us -> 22.4 us
  between operations: 13.6 us -> 0.08 us
  starting transfers between devices: 21.6 us -> 29.9 us
  other arithmetic: 9.84 us -> 2.29 us
    all_to_all x1 -> x0, blocking collectives: 237 us -> none  [local(): lax.all_to_all(group_term.reshape(all_windows, per_device * model_width),...]
    reduce_scatter x1 -> x0, waiting for transfers between devices: 41.7 us -> none  [local(): lax.psum_scatter(picked.astype(jnp.bfloat16), 'pos', scatter_dimension=1,...]
    reshape x6 -> x0, local copies, waits for them, and re-layouts: 40.2 us -> none  [the longest x1 14.8 us: local(): returned = lax.all_to_all(group_term.reshape(all_windows, per_device * mo...]
    all_to_all x2, waiting for transfers between devices: 87.7 us -> 47.8 us  [the longest x1 47.8 us: local(): lax.all_to_all(sent.reshape(X_COUNT * PLANE, 2 * WINDOWS, SLOT), ('x', 'y...]
    dot_general x6 -> x0, matrix products: 33.4 us -> none  [the longest x1 8.24 us: local(): jnp.dot(flat_attended.reshape(all_windows * per_device, group_width), w_o...]
    all_to_all x2 -> x0, local copies, waits for them, and re-layouts: 28.5 us -> none  [local(): lax.all_to_all(group_term.reshape(all_windows, per_device * model_width),...]
    pallas_call x0 -> x3, Pallas kernels: none -> 22.4 us  [the longest x1 12.5 us: project(): pl.pallas_call(project_kernel, in_specs=[HBM, HBM, HBM, HBM], out_specs=H...]
    ppermute x0 -> x5, waiting for transfers between devices: none -> 17 us  [shift(): lax.ppermute(value, axis, [(i, (i + by) % count) for i in range(count)])]
  transfers between devices with their start and end apart: 3 -> 7, of which waited for: 2 -> 4; matrix products, arithmetic and copies ran while one was open for 6% -> 2% of each run, Pallas kernels for 0% -> 4%
where the time goes in v2:
time: 124 us; the launch traced here: 122 us
  waiting for transfers between devices  64.8 us (52%)
  starting transfers between devices  29.9 us (24%)
  Pallas kernels  22.4 us (18%)
  local copies, waits for them, and re-layouts  2.4 us (2%)
  other arithmetic  2.29 us (2%)
    all_to_all x1, waiting for transfers between devices, local(): lax.all_to_all(sent.reshape(X_COUNT * PLANE, 2 * WINDOWS, SLOT), ('x', 'y...  47.8 us
    ppermute x5, waiting for transfers between devices, shift(): lax.ppermute(value, axis, [(i, (i + by) % count) for i in range(count)])  17 us
    all_to_all x1, starting transfers between devices, local(): lax.all_to_all(sent.reshape(X_COUNT * PLANE, 2 * WINDOWS, SLOT), ('x', 'y...  15.4 us
    pallas_call x1, Pallas kernels, project(): pl.pallas_call(project_kernel, in_specs=[HBM, HBM, HBM, HBM], out_specs=H...  12.5 us
    all_to_all x1, starting transfers between devices, local(): lax.all_to_all(attended, ('y', 'z'), split_axis=0, concat_axis=0, tiled=T...  7.43 us
    ppermute x5, starting transfers between devices, shift(): lax.ppermute(value, axis, [(i, (i + by) % count) for i in range(count)])  7.08 us
    pallas_call x1, Pallas kernels, finish(): pl.pallas_call(finish_kernel, in_specs=[VMEM] + [HBM] * 6, out_specs=(VME...  5.31 us
    pallas_call x1, Pallas kernels, attend(): pl.pallas_call(attend_kernel, in_specs=[VMEM], out_specs=VMEM, out_shape=...  4.57 us
  transfers between devices with their start and end apart: 7, of which 4 were waited for; matrix products, arithmetic and copies ran while one was open for 2% of the time, Pallas kernels for 4%

profile of v2, /device:TPU:8, one launch (start us, length us, event | category | flops | bytes accessed | tf_op | source)
XLA Modules:
  0.0 121.9 jit_solution(10250349237383627261)
XLA Ops:
  0.0 12.5 %shard_map.55 = bf16[128,2,8,512]{3,2,1,0:T(8,128)(2,1)} custom-call(bf16[8,128,2560]{2,1,0:T(8,128)(2,1)} %tokens_hbm.3, s32[8,128]{1,0:T(8,128)} %keep_hbm.1, f32[2560]{0:T(1024)} %gain_hbm.1, bf16[3,320,2560]{2,1,0:T(8,128)(2,1)} %w_hbm.1), custom_call_target="tpu_custom_call" | custom-call | flops 5368709120 | bytes 14000000 | tf_op jit(solution)/shard_map/pallas_call | solution.py:126
  12.5 15.4 %all-to-all-start = ((bf16[128,16,512]{2,1,0:T(8,128)(2,1)}), bf16[128,16,512]{2,1,0:T(8,128)(2,1)S(1)}, u32[]{:S(2)}, u32[]{:S(2)}) async-start(bf16[128,16,512]{2,1,0:T(8,128)(2,1)} %bitcast.3), calls=%async_computation | async-start | bytes 4194304 | tf_op jit(solution)/shard_map/all_to_all | solution.py:266
  27.9 1.7 %collective-permute-start = (bf16[320,2560]{1,0:T(8,128)(2,1)}, bf16[320,2560]{1,0:T(8,128)(2,1)}, u32[]{:S(2)}, u32[]{:S(2)}) collective-permute-start(bf16[320,2560]{1,0:T(8,128)(2,1)} %w0.1), channel_id=1, source_target_pairs={{0,2},{2,4},{4,6},{6,0},{1,3},{3,5},{5,7},{7,1},{8,10},{10,12},{12... | collective-permute-start | bytes 4915208 | tf_op jit(solution)/shard_map/ppermute | solution.py:257
  29.6 1.9 %collective-permute-start.2 = (bf16[320,2560]{1,0:T(8,128)(2,1)}, bf16[320,2560]{1,0:T(8,128)(2,1)}, u32[]{:S(2)}, u32[]{:S(2)}) collective-permute-start(bf16[320,2560]{1,0:T(8,128)(2,1)} %w0.1), channel_id=1, source_target_pairs={{0,6},{2,0},{4,2},{6,4},{1,7},{3,1},{5,3},{7,5},{8,14},{10,8},{12,... | collective-permute-start | bytes 4915208 | tf_op jit(solution)/shard_map/ppermute | solution.py:257
  31.5 47.8 %all-to-all-done = bf16[128,16,512]{2,1,0:T(8,128)(2,1)S(1)} async-done(((bf16[128,16,512]{2,1,0:T(8,128)(2,1)}), bf16[128,16,512]{2,1,0:T(8,128)(2,1)S(1)}, u32[]{:S(2)}, u32[]{:S(2)}) %all-to-all-start) | async-done | bytes 2097184 | tf_op jit(solution)/shard_map/all_to_all | solution.py:266
  79.3 4.6 %shard_map.56 = bf16[32,8,1280]{2,1,0:T(8,128)(2,1)} custom-call(bf16[4,32,2,8,512]{4,3,2,1,0:T(8,128)(2,1)S(1)} %bitcast.2), custom_call_target="tpu_custom_call" | custom-call | flops 536870912 | bytes 2800000 | tf_op jit(solution)/shard_map/pallas_call | solution.py:177
  83.9 7.4 %all-to-all-start.1 = ((bf16[32,8,1280]{2,1,0:T(8,128)(2,1)}), bf16[32,8,1280]{2,1,0:T(8,128)(2,1)S(1)}, u32[]{:S(2)}, u32[]{:S(2)}) async-start(bf16[32,8,1280]{2,1,0:T(8,128)(2,1)} %shard_map.56), calls=%async_computation.1 | async-start | bytes 1310720 | tf_op jit(solution)/shard_map/all_to_all | solution.py:270
  91.3 0.0 collective-permute-done.w1
  91.4 1.2 slice.8
  92.6 0.1 collective-permute-start.1
  92.6 0.0 collective-permute-done.2.w3
  92.7 1.2 slice.9
  93.9 3.3 %collective-permute-start.3 = (bf16[160,2560]{1,0:T(8,128)(2,1)S(1)}, bf16[160,2560]{1,0:T(8,128)(2,1)S(1)}, u32[]{:S(2)}, u32[]{:S(2)}) collective-permute-start(bf16[160,2560]{1,0:T(8,128)(2,1)S(1)} %slice.9), channel_id=1, source_target_pairs={{0,6},{2,0},{4,2},{6,4},{1,7},{3,1},{5,3},{7,5},{8,14},{10,8},{12,... | collective-permute-start | bytes 2457608 | tf_op jit(solution)/shard_map/ppermute | solution.py:257
  97.2 14.4 %collective-permute-done.1.w2a = bf16[160,2560]{1,0:T(8,128)(2,1)S(1)} collective-permute-done((bf16[160,2560]{1,0:T(8,128)(2,1)S(1)}, bf16[160,2560]{1,0:T(8,128)(2,1)S(1)}, u32[]{:S(2)}, u32[]{:S(2)}) %collective-permute-start.1) | collective-permute-done | bytes 819232 | tf_op jit(solution)/shard_map/ppermute | solution.py:257
  111.5 0.5 collective-permute-done.3.w2b
  112.1 0.0 all-to-all-done.1.attended_ref
  112.1 5.3 %shard_map.57 = (f32[8,16,2560]{2,1,0:T(8,128)}, bf16[8,16,2560]{2,1,0:T(8,128)(2,1)S(1)}) custom-call(bf16[32,8,1280]{2,1,0:T(8,128)(2,1)S(1)} %all-to-all-done.1.attended_ref, bf16[320,2560]{1,0:T(8,128)(2,1)} %w0.1, bf16[320,2560]{1,0:T(8,128)(2,1)} %collective-permute-done.w1, bf16[160,2560]{1,0:T(8,128)(2,1)S(1)} %collective-permute-done.1.w2a, ...), custom_call_target="tpu_custom_call" | custom-call | flops 1677721600 | bytes 9000000 | tf_op jit(solution)/shard_map/pallas_call | solution.py:235
  117.4 0.1 collective-permute-start.4
  117.5 2.1 %collective-permute-done.4 = bf16[8,16,2560]{2,1,0:T(8,128)(2,1)S(1)} collective-permute-done((bf16[8,16,2560]{2,1,0:T(8,128)(2,1)S(1)}, bf16[8,16,2560]{2,1,0:T(8,128)(2,1)S(1)}, u32[]{:S(2)}, u32[]{:S(2)}) %collective-permute-start.4) | collective-permute-done | bytes 655392 | tf_op jit(solution)/shard_map/ppermute | solution.py:257
  119.6 2.3 %add_convert_fusion = bf16[8,16,2560]{2,1,0:T(8,128)(2,1)} fusion(f32[8,16,2560]{2,1,0:T(8,128)} %get-tuple-element.7, bf16[8,16,2560]{2,1,0:T(8,128)(2,1)S(1)} %collective-permute-done.4), kind=kLoop, calls=%fused_computation | loop fusion | flops 983040 | bytes 2621440 | tf_op jit(solution)/shard_map/convert_element_type | solution.py:272
Async XLA Ops:
  12.5 66.8 %all-to-all-start = ((bf16[128,16,512]{2,1,0:T(8,128)(2,1)}), bf16[128,16,512]{2,1,0:T(8,128)(2,1)S(1)}, u32[]{:S(2)}, u32[]{:S(2)}) async-start(bf16[128,16,512]{2,1,0:T(8,128)(2,1)} %bitcast.3), calls=%async_computation | async-start | bytes 4194304 | tf_op jit(solution)/shard_map/all_to_all | solution.py:266
  27.9 63.4 %collective-permute-start = (bf16[320,2560]{1,0:T(8,128)(2,1)}, bf16[320,2560]{1,0:T(8,128)(2,1)}, u32[]{:S(2)}, u32[]{:S(2)}) collective-permute-start(bf16[320,2560]{1,0:T(8,128)(2,1)} %w0.1), channel_id=1, source_target_pairs={{0,2},{2,4},{4,6},{6,0},{1,3},{3,5},{5,7},{7,1},{8,10},{10,12},{12... | collective-permute-start | bytes 4915208 | tf_op jit(solution)/shard_map/ppermute | solution.py:257
  29.6 63.1 %collective-permute-start.2 = (bf16[320,2560]{1,0:T(8,128)(2,1)}, bf16[320,2560]{1,0:T(8,128)(2,1)}, u32[]{:S(2)}, u32[]{:S(2)}) collective-permute-start(bf16[320,2560]{1,0:T(8,128)(2,1)} %w0.1), channel_id=1, source_target_pairs={{0,6},{2,0},{4,2},{6,4},{1,7},{3,1},{5,3},{7,5},{8,14},{10,8},{12,... | collective-permute-start | bytes 4915208 | tf_op jit(solution)/shard_map/ppermute | solution.py:257
  83.9 28.2 %all-to-all-start.1 = ((bf16[32,8,1280]{2,1,0:T(8,128)(2,1)}), bf16[32,8,1280]{2,1,0:T(8,128)(2,1)S(1)}, u32[]{:S(2)}, u32[]{:S(2)}) async-start(bf16[32,8,1280]{2,1,0:T(8,128)(2,1)} %shard_map.56), calls=%async_computation.1 | async-start | bytes 1310720 | tf_op jit(solution)/shard_map/all_to_all | solution.py:270
  92.6 19.0 %collective-permute-start.1 = (bf16[160,2560]{1,0:T(8,128)(2,1)S(1)}, bf16[160,2560]{1,0:T(8,128)(2,1)S(1)}, u32[]{:S(2)}, u32[]{:S(2)}) collective-permute-start(bf16[160,2560]{1,0:T(8,128)(2,1)S(1)} %slice.8), channel_id=1, source_target_pairs={{0,2},{2,4},{4,6},{6,0},{1,3},{3,5},{5,7},{7,1},{8,10},{10,12},{12... | collective-permute-start | bytes 2457608 | tf_op jit(solution)/shard_map/ppermute | solution.py:257
  93.9 18.2 %collective-permute-start.3 = (bf16[160,2560]{1,0:T(8,128)(2,1)S(1)}, bf16[160,2560]{1,0:T(8,128)(2,1)S(1)}, u32[]{:S(2)}, u32[]{:S(2)}) collective-permute-start(bf16[160,2560]{1,0:T(8,128)(2,1)S(1)} %slice.9), channel_id=1, source_target_pairs={{0,6},{2,0},{4,2},{6,4},{1,7},{3,1},{5,3},{7,5},{8,14},{10,8},{12,... | collective-permute-start | bytes 2457608 | tf_op jit(solution)/shard_map/ppermute | solution.py:257
  117.4 2.2 %collective-permute-start.4 = (bf16[8,16,2560]{2,1,0:T(8,128)(2,1)S(1)}, bf16[8,16,2560]{2,1,0:T(8,128)(2,1)S(1)}, u32[]{:S(2)}, u32[]{:S(2)}) collective-permute-start(bf16[8,16,2560]{2,1,0:T(8,128)(2,1)S(1)} %get-tuple-element.8), channel_id=1, source_target_pairs={{0,1},{1,0},{2,3},{3,2},{4,5},{5,4},{6,7},{7,6},{8,9},{9,8},{10,11... | collective-permute-start | bytes 1966088 | tf_op jit(solution)/shard_map/ppermute | solution.py:257

commit v3 on v2

--- a/solution.py
+++ b/solution.py
@@ -15,8 +15,9 @@
 WINDOWS = 8
 PAIRS = 128
 SLOT = 512
-FLAG = 3 * HEAD_DIM
 LAST = SLOT - 128
+TAIL = HEAD_DIM - 128
+FLAG = 3 * TAIL
 X_COUNT = 4
 PLANE = 32
 
@@ -38,11 +39,10 @@
         for b in range(BLOCKS)
     ]
     w_copies = [
-        [
+        [pltpu.make_async_copy(w_hbm.at[:, h, pl.ds(0, 128)], w_ref.at[h, pl.ds(0, 3)], sems.at[BLOCKS + h, 3])]
+        + [
             pltpu.make_async_copy(
-                w_hbm.at[c, pl.ds(h * HEAD_DIM, HEAD_DIM)],
-                w_ref.at[pl.ds(h * SLOT + c * HEAD_DIM, HEAD_DIM)],
-                sems.at[BLOCKS + h, c],
+                w_hbm.at[c, h, pl.ds(128, TAIL)], w_ref.at[h, 3, pl.ds(c * TAIL, TAIL)], sems.at[BLOCKS + h, c]
             )
             for c in range(3)
         ]
@@ -61,7 +61,7 @@
         copy.start()
     keep_copy.start()
     for h in range(2):
-        w_ref[h * SLOT + FLAG:(h + 1) * SLOT, :] = jnp.zeros((SLOT - FLAG, D), BF16)
+        w_ref[h, 3, FLAG:, :] = jnp.zeros((128 - FLAG, D), BF16)
     gain_copy.wait()
     gain = gain_ref[...].reshape(1, D)
 
@@ -95,7 +95,7 @@
                     copy.wait()
             part = lax.dot_general(
                 rows_refs[b][...],
-                w_ref[h * SLOT:(h + 1) * SLOT, :],
+                w_ref[h].reshape(SLOT, D),
                 (((1,), (1,)), ((), ())),
                 preferred_element_type=F32,
             )
@@ -104,7 +104,7 @@
                 piece = part[:, lanes]
                 if c == LAST // 128:
                     piece = jnp.where(
-                        lane == FLAG - LAST, odd, jnp.where(lane == FLAG - LAST + 1, 1.0 - odd, piece)
+                        lane == FLAG, odd, jnp.where(lane == FLAG + 1, 1.0 - odd, piece)
                     )
                 at = h * (SLOT // 128) + c
                 for w in range(WINDOWS):
@@ -133,44 +133,64 @@
             pltpu.VMEM((D,), F32),
             pltpu.VMEM((BLOCKS, WINDOWS, BLOCK, D), BF16),
             pltpu.VMEM((WINDOWS, PAIRS), jnp.int32),
-            pltpu.VMEM((2 * SLOT, D), BF16),
+            pltpu.VMEM((2, 4, 128, D), BF16),
             pltpu.VMEM((2, 2 * SLOT // 128, rows, 128), F32),
         ]
         + [pltpu.VMEM((rows, D), BF16)] * BLOCKS
         + [pltpu.SemaphoreType.DMA((BLOCKS + 3, WINDOWS))],
         compiler_params=pltpu.CompilerParams(vmem_limit_bytes=LIMIT),
         cost_estimate=pl.CostEstimate(flops=2 * 1024 * 1024 * D, bytes_accessed=14_000_000, transcendentals=0),
-    )(tokens, keep_index, norm_gain, w_qkv)
+    )(tokens, keep_index, norm_gain, w_qkv.reshape(3, 2, HEAD_DIM, D))
+
+
+BATCH = 4
 
 
 def attend_kernel(in_ref, out_ref):
     total = PLANE * WINDOWS
     scale = 1.0 / math.sqrt(HEAD_DIM)
+    lane = lax.broadcasted_iota(jnp.int32, (total, 128), 1)
     flags = in_ref[0, :, 0, :, LAST:].astype(F32).reshape(total, 128)
-    lane = lax.broadcasted_iota(jnp.int32, flags.shape, 1)
-    flags = jnp.where(lane >= FLAG - LAST, flags, 0.0).astype(BF16)
+    flags = jnp.where(lane >= FLAG, flags, 0.0).astype(BF16)
     same = lax.dot_general(flags, flags, (((1,), (1,)), ((), ())), preferred_element_type=F32) > 0.5
     me = lax.axis_index("x")
-    heads, tails = [], []
-    for d in range(X_COUNT):
-        source = lax.rem(me - d + X_COUNT, X_COUNT)
-        group = []
-        for h in range(2):
-            block = in_ref[source, :, h].astype(F32).reshape(total, SLOT).astype(BF16)
-            query = block[:, :HEAD_DIM]
-            key = block[:, HEAD_DIM:2 * HEAD_DIM]
-            value = block[:, 2 * HEAD_DIM:3 * HEAD_DIM]
-            scores = lax.dot_general(query, key, (((1,), (1,)), ((), ())), preferred_element_type=F32) * scale
-            scores = jnp.where(same, scores, -jnp.inf)
-            top = jnp.max(scores, axis=-1, keepdims=True)
-            exponent = jnp.exp(scores - top)
-            weights = exponent * (1.0 / jnp.sum(exponent, axis=-1, keepdims=True))
-            group.append(jnp.dot(weights.astype(BF16), value, preferred_element_type=F32))
-        group = jnp.concatenate(group, axis=-1)
-        heads.append(group[:, :256])
-        tails.append(group[:, 256:])
-    attended = jnp.concatenate(heads + tails, axis=-1)
-    out_ref[...] = attended.reshape(PLANE, WINDOWS, X_COUNT * GROUP).astype(BF16)
+    units = [(d, h) for d in range(X_COUNT) for h in range(2)]
+    tails = []
+    for first in range(0, 8, BATCH):
+        group = units[first:first + BATCH]
+        scores, values = [], []
+        for d, h in group:
+            source = lax.rem(me - d + X_COUNT, X_COUNT)
+
+            def part(i):
+                return in_ref[source, :, h, :, i * 128:(i + 1) * 128].astype(F32).reshape(total, 128)
+
+            last = part(3)
+            query = jnp.concatenate([part(0), jnp.where(lane < TAIL, last, 0.0)], axis=-1).astype(BF16)
+            key = jnp.concatenate([part(1), pltpu.roll(last, 128 - TAIL, 1)], axis=-1).astype(BF16)
+            value_tail = jnp.where(lane < TAIL, pltpu.roll(last, 128 - 2 * TAIL, 1), 1.0)
+            values.append(jnp.concatenate([part(2), value_tail], axis=-1).astype(BF16))
+            scores.append(lax.dot_general(query, key, (((1,), (1,)), ((), ())), preferred_element_type=F32))
+        weights = []
+        for score in scores:
+            score = jnp.where(same, score * scale, -jnp.inf)
+            weights.append(jnp.exp(score - jnp.max(score, axis=-1, keepdims=True)).astype(BF16))
+        mixes = [jnp.dot(w, v, preferred_element_type=F32) for w, v in zip(weights, values)]
+        for (d, h), mixed in zip(group, mixes):
+            unit = d * 2 + h
+            scaled = mixed * (1.0 / mixed[:, 128 + TAIL:128 + TAIL + 1])
+            out_ref[:, :, unit * 128:(unit + 1) * 128] = scaled[:, :128].reshape(PLANE, WINDOWS, 128).astype(BF16)
+            tail = scaled[:, 128:]
+            place = unit % 4
+            if place == 0:
+                gathered = tail
+            else:
+                gathered = jnp.where(lane < place * TAIL, gathered, pltpu.roll(tail, place * TAIL, 1))
+            if place == 3:
+                tails.append(gathered)
+    for i, tail in enumerate(tails):
+        at = 1024 + i * 128
+        out_ref[:, :, at:at + 128] = tail.reshape(PLANE, WINDOWS, 128).astype(BF16)
 
 
 def attend(received):
@@ -188,22 +208,21 @@
 CHUNKS = D // CHUNK
 
 
-def finish_kernel(attended_ref, w0, w1, w2a, w2b, w3, tokens_hbm, own_ref, other_ref, w_ref, t_ref, x_ref, rows_ref, sems):
+def finish_kernel(attended_ref, w0, w1, w2a, w2b, w3, tokens_hbm, own_ref, other_ref, *scratch):
+    w_ref, w_tail_ref, t_ref, x_ref, rows_ref, sems = scratch
     core = lax.axis_index("c")
     first = pl.multiple_of((lax.axis_index("x") * 2 + core) * 16, 16)
     token_copy = pltpu.make_async_copy(tokens_hbm.at[:, pl.ds(first, 16)], t_ref, sems.at[CHUNKS, 0])
-    parts = []
-    for d, w in ((0, w0), (1, w1), (3, w3)):
-        parts += [(w, 0, 256, d * 256), (w, 256, 64, 1024 + d * 64)]
-    parts += [(w2a, 0, 160, 512), (w2b, 0, 96, 672), (w2b, 96, 64, 1152)]
+    parts = [(w0, 0), (w1, 2), (w2a, 4), (w2b, 5), (w3, 6)]
     copies = [
         [
             pltpu.make_async_copy(
-                w.at[pl.ds(lo, size), pl.ds(n * CHUNK, CHUNK)],
-                w_ref.at[pl.ds(to, size), pl.ds(n * CHUNK, CHUNK)],
-                sems.at[n, i],
+                w.at[:, pl.ds(lo, size), pl.ds(n * CHUNK, CHUNK)],
+                to_ref.at[pl.ds(head, w.shape[0]), :, pl.ds(n * CHUNK, CHUNK)],
+                sems.at[n, i * 2 + j],
             )
-            for i, (w, lo, size, to) in enumerate(parts)
+            for i, (w, head) in enumerate(parts)
+            for j, (lo, size, to_ref) in enumerate(((0, 128, w_ref), (128, TAIL, w_tail_ref)))
         ]
         for n in range(CHUNKS)
     ]
@@ -224,7 +243,9 @@
         lanes = slice(n * CHUNK, (n + 1) * CHUNK)
         for copy in copies[n]:
             copy.wait()
-        total = jnp.dot(rows_ref[...], w_ref[:, lanes], preferred_element_type=F32)
+        total = jnp.dot(
+            rows_ref[:, :1024], w_ref[:, :, lanes].reshape(1024, CHUNK), preferred_element_type=F32
+        ) + jnp.dot(rows_ref[:, 1024:], w_tail_ref[:, :, lanes].reshape(256, CHUNK), preferred_element_type=F32)
         if n == 0:
             token_copy.wait()
         own_ref[:, :, lanes] = t_ref[:, :, lanes].astype(F32) + total[:128].reshape(WINDOWS, 16, CHUNK)
@@ -241,15 +262,16 @@
             jax.ShapeDtypeStruct((WINDOWS, 16, D), BF16),
         ),
         scratch_shapes=[
-            pltpu.VMEM((X_COUNT * GROUP, D), BF16),
+            pltpu.VMEM((8, 128, D), BF16),
+            pltpu.VMEM((8, TAIL, D), BF16),
             pltpu.VMEM((WINDOWS, 16, D), BF16),
             pltpu.VMEM((X_COUNT * GROUP // 128, PLANE * WINDOWS, 128), F32),
             pltpu.VMEM((PLANE * WINDOWS, X_COUNT * GROUP), BF16),
-            pltpu.SemaphoreType.DMA((CHUNKS + 1, 9)),
+            pltpu.SemaphoreType.DMA((CHUNKS + 1, 10)),
         ],
         compiler_params=pltpu.CompilerParams(vmem_limit_bytes=50 * 1024 * 1024),
         cost_estimate=pl.CostEstimate(flops=2 * 256 * 1280 * D, bytes_accessed=9_000_000, transcendentals=0),
-    )(attended, *weights, tokens)
+    )(attended, *[w.reshape(-1, HEAD_DIM, D) for w in weights], tokens)
 
 
 def shift(value, axis, by):

time: 124 us -> 123 us (level)
  Pallas kernels: 22.4 us -> 20.4 us
    pallas_call x1, Pallas kernels: 4.57 us -> 2.51 us  [attend(): pl.pallas_call(attend_kernel, in_specs=[VMEM], out_specs=VMEM, out_shape=...]
  transfers between devices with their start and end apart: 7 -> 7, of which waited for: 4 -> 4; matrix products, arithmetic and copies ran while one was open for 2% -> 2% of each run, Pallas kernels for 4% -> 2%
where the time goes in v3:
time: 123 us; the launch traced here: 121 us
  waiting for transfers between devices  65.7 us (53%)
  starting transfers between devices  29.9 us (24%)
  Pallas kernels  20.4 us (17%)
  local copies, waits for them, and re-layouts  2.4 us (2%)
  other arithmetic  2.29 us (2%)
    all_to_all x1, waiting for transfers between devices, local(): lax.all_to_all(sent.reshape(X_COUNT * PLANE, 2 * WINDOWS, SLOT), ('x', 'y...  47.8 us
    ppermute x5, waiting for transfers between devices, shift(): lax.ppermute(value, axis, [(i, (i + by) % count) for i in range(count)])  17.9 us
    all_to_all x1, starting transfers between devices, local(): lax.all_to_all(sent.reshape(X_COUNT * PLANE, 2 * WINDOWS, SLOT), ('x', 'y...  15.4 us
    pallas_call x1, Pallas kernels, project(): pl.pallas_call(project_kernel, in_specs=[HBM, HBM, HBM, HBM], out_specs=H...  12.5 us
    all_to_all x1, starting transfers between devices, local(): lax.all_to_all(attended, ('y', 'z'), split_axis=0, concat_axis=0, tiled=T...  7.43 us
    ppermute x5, starting transfers between devices, shift(): lax.ppermute(value, axis, [(i, (i + by) % count) for i in range(count)])  7.08 us
    pallas_call x1, Pallas kernels, finish(): pl.pallas_call(finish_kernel, in_specs=[VMEM] + [HBM] * 6, out_specs=(VME...  5.38 us
    pallas_call x1, Pallas kernels, attend(): pl.pallas_call(attend_kernel, in_specs=[VMEM], out_specs=VMEM, out_shape=...  2.51 us
  transfers between devices with their start and end apart: 7, of which 4 were waited for; matrix products, arithmetic and copies ran while one was open for 2% of the time, Pallas kernels for 2%

profile of v3, /device:TPU:8, one launch (start us, length us, event | category | flops | bytes accessed | tf_op | source)
XLA Modules:
  0.0 120.8 jit_solution(14653696529975978941)
XLA Ops:
  0.0 12.5 %shard_map.55 = bf16[128,2,8,512]{3,2,1,0:T(8,128)(2,1)} custom-call(bf16[8,128,2560]{2,1,0:T(8,128)(2,1)} %tokens_hbm.3, s32[8,128]{1,0:T(8,128)} %keep_hbm.1, f32[2560]{0:T(1024)} %gain_hbm.1, bf16[3,2,160,2560]{3,2,1,0:T(8,128)(2,1)} %bitcast.13), custom_call_target="tpu_custom_call" | custom-call | flops 5368709120 | bytes 14000000 | tf_op jit(solution)/shard_map/pallas_call | solution.py:126
  12.5 15.4 %all-to-all-start = ((bf16[128,16,512]{2,1,0:T(8,128)(2,1)}), bf16[128,16,512]{2,1,0:T(8,128)(2,1)S(1)}, u32[]{:S(2)}, u32[]{:S(2)}) async-start(bf16[128,16,512]{2,1,0:T(8,128)(2,1)} %bitcast.11), calls=%async_computation | async-start | bytes 4194304 | tf_op jit(solution)/shard_map/all_to_all | solution.py:288
  27.9 1.7 %collective-permute-start = (bf16[320,2560]{1,0:T(8,128)(2,1)}, bf16[320,2560]{1,0:T(8,128)(2,1)}, u32[]{:S(2)}, u32[]{:S(2)}) collective-permute-start(bf16[320,2560]{1,0:T(8,128)(2,1)} %param.9), channel_id=1, source_target_pairs={{0,2},{2,4},{4,6},{6,0},{1,3},{3,5},{5,7},{7,1},{8,10},{10,12},{12... | collective-permute-start | bytes 4915208 | tf_op jit(solution)/shard_map/ppermute | solution.py:279
  29.6 1.9 %collective-permute-start.2 = (bf16[320,2560]{1,0:T(8,128)(2,1)}, bf16[320,2560]{1,0:T(8,128)(2,1)}, u32[]{:S(2)}, u32[]{:S(2)}) collective-permute-start(bf16[320,2560]{1,0:T(8,128)(2,1)} %param.9), channel_id=1, source_target_pairs={{0,6},{2,0},{4,2},{6,4},{1,7},{3,1},{5,3},{7,5},{8,14},{10,8},{12,... | collective-permute-start | bytes 4915208 | tf_op jit(solution)/shard_map/ppermute | solution.py:279
  31.5 47.8 %all-to-all-done = bf16[128,16,512]{2,1,0:T(8,128)(2,1)S(1)} async-done(((bf16[128,16,512]{2,1,0:T(8,128)(2,1)}), bf16[128,16,512]{2,1,0:T(8,128)(2,1)S(1)}, u32[]{:S(2)}, u32[]{:S(2)}) %all-to-all-start) | async-done | bytes 2097184 | tf_op jit(solution)/shard_map/all_to_all | solution.py:288
  79.3 2.5 %shard_map.56 = bf16[32,8,1280]{2,1,0:T(8,128)(2,1)} custom-call(bf16[4,32,2,8,512]{4,3,2,1,0:T(8,128)(2,1)S(1)} %bitcast.8), custom_call_target="tpu_custom_call" | custom-call | flops 536870912 | bytes 2800000 | tf_op jit(solution)/shard_map/pallas_call | solution.py:197
  81.9 7.4 %all-to-all-start.1 = ((bf16[32,8,1280]{2,1,0:T(8,128)(2,1)}), bf16[32,8,1280]{2,1,0:T(8,128)(2,1)S(1)}, u32[]{:S(2)}, u32[]{:S(2)}) async-start(bf16[32,8,1280]{2,1,0:T(8,128)(2,1)} %shard_map.56), calls=%async_computation.1 | async-start | bytes 1310720 | tf_op jit(solution)/shard_map/all_to_all | solution.py:292
  89.3 0.0 collective-permute-done
  89.3 1.2 slice.8
  90.5 0.1 collective-permute-start.1
  90.6 0.0 collective-permute-done.2
  90.6 1.2 slice.9
  91.8 3.3 %collective-permute-start.3 = (bf16[160,2560]{1,0:T(8,128)(2,1)S(1)}, bf16[160,2560]{1,0:T(8,128)(2,1)S(1)}, u32[]{:S(2)}, u32[]{:S(2)}) collective-permute-start(bf16[160,2560]{1,0:T(8,128)(2,1)S(1)} %slice.9), channel_id=1, source_target_pairs={{0,6},{2,0},{4,2},{6,4},{1,7},{3,1},{5,3},{7,5},{8,14},{10,8},{12,... | collective-permute-start | bytes 2457608 | tf_op jit(solution)/shard_map/ppermute | solution.py:279
  95.1 15.2 %collective-permute-done.1 = bf16[160,2560]{1,0:T(8,128)(2,1)S(1)} collective-permute-done((bf16[160,2560]{1,0:T(8,128)(2,1)S(1)}, bf16[160,2560]{1,0:T(8,128)(2,1)S(1)}, u32[]{:S(2)}, u32[]{:S(2)}) %collective-permute-start.1) | collective-permute-done | bytes 819232 | tf_op jit(solution)/shard_map/ppermute | solution.py:279
  110.3 0.5 collective-permute-done.3
  110.9 0.0 all-to-all-done.1.attended_ref
  110.9 5.4 %shard_map.57 = (f32[8,16,2560]{2,1,0:T(8,128)}, bf16[8,16,2560]{2,1,0:T(8,128)(2,1)S(1)}) custom-call(bf16[32,8,1280]{2,1,0:T(8,128)(2,1)S(1)} %all-to-all-done.1.attended_ref, bf16[2,160,2560]{2,1,0:T(8,128)(2,1)} %bitcast.12, bf16[2,160,2560]{2,1,0:T(8,128)(2,1)} %bitcast.4.w1, bf16[1,160,2560]{2,1,0:T(8,128)(2,1)S(1)} %bitcast.9, ...), custom_call_target="tpu_custom_call" | custom-call | flops 1677721600 | bytes 9000000 | tf_op jit(solution)/shard_map/pallas_call | solution.py:256
  116.3 0.1 collective-permute-start.4
  116.4 2.1 %collective-permute-done.4 = bf16[8,16,2560]{2,1,0:T(8,128)(2,1)S(1)} collective-permute-done((bf16[8,16,2560]{2,1,0:T(8,128)(2,1)S(1)}, bf16[8,16,2560]{2,1,0:T(8,128)(2,1)S(1)}, u32[]{:S(2)}, u32[]{:S(2)}) %collective-permute-start.4) | collective-permute-done | bytes 655392 | tf_op jit(solution)/shard_map/ppermute | solution.py:279
  118.5 2.3 %add_convert_fusion = bf16[8,16,2560]{2,1,0:T(8,128)(2,1)} fusion(f32[8,16,2560]{2,1,0:T(8,128)} %get-tuple-element.7, bf16[8,16,2560]{2,1,0:T(8,128)(2,1)S(1)} %collective-permute-done.4), kind=kLoop, calls=%fused_computation | loop fusion | flops 983040 | bytes 2621440 | tf_op jit(solution)/shard_map/convert_element_type | solution.py:294
Async XLA Ops:
  12.5 66.8 %all-to-all-start = ((bf16[128,16,512]{2,1,0:T(8,128)(2,1)}), bf16[128,16,512]{2,1,0:T(8,128)(2,1)S(1)}, u32[]{:S(2)}, u32[]{:S(2)}) async-start(bf16[128,16,512]{2,1,0:T(8,128)(2,1)} %bitcast.11), calls=%async_computation | async-start | bytes 4194304 | tf_op jit(solution)/shard_map/all_to_all | solution.py:288
  27.9 61.4 %collective-permute-start = (bf16[320,2560]{1,0:T(8,128)(2,1)}, bf16[320,2560]{1,0:T(8,128)(2,1)}, u32[]{:S(2)}, u32[]{:S(2)}) collective-permute-start(bf16[320,2560]{1,0:T(8,128)(2,1)} %param.9), channel_id=1, source_target_pairs={{0,2},{2,4},{4,6},{6,0},{1,3},{3,5},{5,7},{7,1},{8,10},{10,12},{12... | collective-permute-start | bytes 4915208 | tf_op jit(solution)/shard_map/ppermute | solution.py:279
  29.6 61.0 %collective-permute-start.2 = (bf16[320,2560]{1,0:T(8,128)(2,1)}, bf16[320,2560]{1,0:T(8,128)(2,1)}, u32[]{:S(2)}, u32[]{:S(2)}) collective-permute-start(bf16[320,2560]{1,0:T(8,128)(2,1)} %param.9), channel_id=1, source_target_pairs={{0,6},{2,0},{4,2},{6,4},{1,7},{3,1},{5,3},{7,5},{8,14},{10,8},{12,... | collective-permute-start | bytes 4915208 | tf_op jit(solution)/shard_map/ppermute | solution.py:279
  81.9 29.0 %all-to-all-start.1 = ((bf16[32,8,1280]{2,1,0:T(8,128)(2,1)}), bf16[32,8,1280]{2,1,0:T(8,128)(2,1)S(1)}, u32[]{:S(2)}, u32[]{:S(2)}) async-start(bf16[32,8,1280]{2,1,0:T(8,128)(2,1)} %shard_map.56), calls=%async_computation.1 | async-start | bytes 1310720 | tf_op jit(solution)/shard_map/all_to_all | solution.py:292
  90.5 19.8 %collective-permute-start.1 = (bf16[160,2560]{1,0:T(8,128)(2,1)S(1)}, bf16[160,2560]{1,0:T(8,128)(2,1)S(1)}, u32[]{:S(2)}, u32[]{:S(2)}) collective-permute-start(bf16[160,2560]{1,0:T(8,128)(2,1)S(1)} %slice.8), channel_id=1, source_target_pairs={{0,2},{2,4},{4,6},{6,0},{1,3},{3,5},{5,7},{7,1},{8,10},{10,12},{12... | collective-permute-start | bytes 2457608 | tf_op jit(solution)/shard_map/ppermute | solution.py:279
  91.8 19.1 %collective-permute-start.3 = (bf16[160,2560]{1,0:T(8,128)(2,1)S(1)}, bf16[160,2560]{1,0:T(8,128)(2,1)S(1)}, u32[]{:S(2)}, u32[]{:S(2)}) collective-permute-start(bf16[160,2560]{1,0:T(8,128)(2,1)S(1)} %slice.9), channel_id=1, source_target_pairs={{0,6},{2,0},{4,2},{6,4},{1,7},{3,1},{5,3},{7,5},{8,14},{10,8},{12,... | collective-permute-start | bytes 2457608 | tf_op jit(solution)/shard_map/ppermute | solution.py:279
  116.3 2.2 %collective-permute-start.4 = (bf16[8,16,2560]{2,1,0:T(8,128)(2,1)S(1)}, bf16[8,16,2560]{2,1,0:T(8,128)(2,1)S(1)}, u32[]{:S(2)}, u32[]{:S(2)}) collective-permute-start(bf16[8,16,2560]{2,1,0:T(8,128)(2,1)S(1)} %get-tuple-element.8), channel_id=1, source_target_pairs={{0,1},{1,0},{2,3},{3,2},{4,5},{5,4},{6,7},{7,6},{8,9},{9,8},{10,11... | collective-permute-start | bytes 1966088 | tf_op jit(solution)/shard_map/ppermute | solution.py:279

commit v4 on v3

--- a/solution.py
+++ b/solution.py
@@ -31,7 +31,7 @@
 BLOCKS = PAIRS // BLOCK
 
 
-def project_kernel(tokens_hbm, keep_hbm, gain_hbm, w_hbm, out_hbm, out_ref, gain_ref, x_ref, keep_ref, w_ref, spread_ref, *rest):
+def project_kernel(tokens_hbm, keep_hbm, gain_hbm, w_hbm, out_hbm, out_ref, gain_ref, x_ref, keep_ref, w_ref, *rest):
     rows_refs, sems = rest[:BLOCKS], rest[BLOCKS]
     rows = WINDOWS * BLOCK
     token_copies = [
@@ -51,9 +51,12 @@
     keep_copy = pltpu.make_async_copy(keep_hbm, keep_ref, sems.at[BLOCKS + 2, 0])
     gain_copy = pltpu.make_async_copy(gain_hbm, gain_ref, sems.at[BLOCKS + 2, 1])
     out_copies = [
-        pltpu.make_async_copy(
-            out_ref.at[pl.ds(b * BLOCK, BLOCK)], out_hbm.at[pl.ds(b * BLOCK, BLOCK)], sems.at[BLOCKS + 2, 2 + b]
-        )
+        [
+            pltpu.make_async_copy(
+                out_ref.at[pl.ds(b * BLOCK, BLOCK), h], out_hbm.at[pl.ds(b * BLOCK, BLOCK), h], sems.at[b, 1 + h]
+            )
+            for h in range(2)
+        ]
         for b in range(BLOCKS)
     ]
     gain_copy.start()
@@ -90,6 +93,10 @@
             token_copies[b + 2].start()
         odd = jnp.sum(jnp.where(row_pair + b * BLOCK == lane, spread, 0.0), axis=-1, keepdims=True)
         for h in range(2):
+            if h == 1 and b + 1 < BLOCKS:
+                token_copies[b + 1].wait()
+                for w in range(WINDOWS):
+                    norm(b + 1, w)
             if b == 0:
                 for copy in w_copies[h]:
                     copy.wait()
@@ -106,19 +113,13 @@
                     piece = jnp.where(
                         lane == FLAG, odd, jnp.where(lane == FLAG + 1, 1.0 - odd, piece)
                     )
-                at = h * (SLOT // 128) + c
-                for w in range(WINDOWS):
-                    spread_ref[b % 2, at, pl.ds(w, BLOCK, stride=WINDOWS), :] = piece[w * BLOCK:(w + 1) * BLOCK]
-                out_ref[b * BLOCK:(b + 1) * BLOCK, h, :, lanes] = (
-                    spread_ref[b % 2, at].reshape(BLOCK, WINDOWS, 128).astype(BF16)
-                )
-        out_copies[b].start()
-        if b + 1 < BLOCKS:
-            token_copies[b + 1].wait()
-            for w in range(WINDOWS):
-                norm(b + 1, w)
-    for copy in out_copies:
-        copy.wait()
+                out_ref[b * BLOCK:(b + 1) * BLOCK, h, :, lanes] = jnp.swapaxes(
+                    piece.reshape(WINDOWS, BLOCK, 128), 0, 1
+                ).astype(BF16)
+            out_copies[b][h].start()
+    for copies in out_copies:
+        for copy in copies:
+            copy.wait()
 
 
 def project(tokens, keep_index, norm_gain, w_qkv):
@@ -134,7 +135,6 @@
             pltpu.VMEM((BLOCKS, WINDOWS, BLOCK, D), BF16),
             pltpu.VMEM((WINDOWS, PAIRS), jnp.int32),
             pltpu.VMEM((2, 4, 128, D), BF16),
-            pltpu.VMEM((2, 2 * SLOT // 128, rows, 128), F32),
         ]
         + [pltpu.VMEM((rows, D), BF16)] * BLOCKS
         + [pltpu.SemaphoreType.DMA((BLOCKS + 3, WINDOWS))],
@@ -154,6 +154,12 @@
     flags = jnp.where(lane >= FLAG, flags, 0.0).astype(BF16)
     same = lax.dot_general(flags, flags, (((1,), (1,)), ((), ())), preferred_element_type=F32) > 0.5
     me = lax.axis_index("x")
+
+    def store(tile, rows):
+        rows = rows.reshape(4, 8, WINDOWS, 128).astype(BF16)
+        for y in range(4):
+            out_ref[:, y, :, tile * 128:(tile + 1) * 128] = rows[y]
+
     units = [(d, h) for d in range(X_COUNT) for h in range(2)]
     tails = []
     for first in range(0, 8, BATCH):
@@ -179,7 +185,7 @@
         for (d, h), mixed in zip(group, mixes):
             unit = d * 2 + h
             scaled = mixed * (1.0 / mixed[:, 128 + TAIL:128 + TAIL + 1])
-            out_ref[:, :, unit * 128:(unit + 1) * 128] = scaled[:, :128].reshape(PLANE, WINDOWS, 128).astype(BF16)
+            store(unit, scaled[:, :128])
             tail = scaled[:, 128:]
             place = unit % 4
             if place == 0:
@@ -189,8 +195,7 @@
             if place == 3:
                 tails.append(gathered)
     for i, tail in enumerate(tails):
-        at = 1024 + i * 128
-        out_ref[:, :, at:at + 128] = tail.reshape(PLANE, WINDOWS, 128).astype(BF16)
+        store(8 + i, tail)
 
 
 def attend(received):
@@ -198,7 +203,7 @@
         attend_kernel,
         in_specs=[VMEM],
         out_specs=VMEM,
-        out_shape=jax.ShapeDtypeStruct((PLANE, WINDOWS, X_COUNT * GROUP), BF16),
+        out_shape=jax.ShapeDtypeStruct((8, 4, WINDOWS, X_COUNT * GROUP), BF16),
         compiler_params=pltpu.CompilerParams(vmem_limit_bytes=48 * 1024 * 1024),
         cost_estimate=pl.CostEstimate(flops=8 * 4 * 256 ** 3, bytes_accessed=2_800_000, transcendentals=8 * 65536),
     )(received)
@@ -208,8 +213,8 @@
 CHUNKS = D // CHUNK
 
 
-def finish_kernel(attended_ref, w0, w1, w2a, w2b, w3, tokens_hbm, own_ref, other_ref, *scratch):
-    w_ref, w_tail_ref, t_ref, x_ref, rows_ref, sems = scratch
+def finish_kernel(attended_ref, w0, w1, w2a, w2b, w3, tokens_hbm, own_hbm, other_hbm, *scratch):
+    w_ref, w_tail_ref, t_ref, x_ref, rows_ref, own_ref, other_ref, sems, out_sems = scratch
     core = lax.axis_index("c")
     first = pl.multiple_of((lax.axis_index("x") * 2 + core) * 16, 16)
     token_copy = pltpu.make_async_copy(tokens_hbm.at[:, pl.ds(first, 16)], t_ref, sems.at[CHUNKS, 0])
@@ -235,10 +240,14 @@
     for c in range(X_COUNT * GROUP // 128):
         lanes = slice(c * 128, (c + 1) * 128)
         x_ref[c] = attended_ref[:, :, lanes].astype(F32).reshape(PLANE * WINDOWS, 128)
-        for half, start in ((0, core * 128), (1, (1 - core) * 128)):
+        for half, owner in ((0, core), (1, 1 - core)):
             for w in range(WINDOWS):
                 to = half * 128 + w * 16
-                rows_ref[to:to + 16, lanes] = x_ref[c, pl.ds(start + w, 16, stride=WINDOWS), :].astype(BF16)
+                picked = [
+                    x_ref[c, pl.ds((owner * 2 + y) * WINDOWS + w, 8, stride=4 * WINDOWS), :] for y in range(2)
+                ]
+                rows_ref[to:to + 16, lanes] = jnp.concatenate(picked, axis=0).astype(BF16)
+    out_copies = []
     for n in range(CHUNKS):
         lanes = slice(n * CHUNK, (n + 1) * CHUNK)
         for copy in copies[n]:
@@ -248,17 +257,26 @@
         ) + jnp.dot(rows_ref[:, 1024:], w_tail_ref[:, :, lanes].reshape(256, CHUNK), preferred_element_type=F32)
         if n == 0:
             token_copy.wait()
-        own_ref[:, :, lanes] = t_ref[:, :, lanes].astype(F32) + total[:128].reshape(WINDOWS, 16, CHUNK)
+        own = t_ref[:, :, lanes].astype(F32) + total[:128].reshape(WINDOWS, 16, CHUNK)
+        own_ref[:, :, lanes] = own.astype(BF16)
         other_ref[:, :, lanes] = total[128:].reshape(WINDOWS, 16, CHUNK).astype(BF16)
+        columns = pl.ds(n * CHUNK, CHUNK)
+        for i, (ref, hbm) in enumerate(((own_ref, own_hbm), (other_ref, other_hbm))):
+            out_copies.append(
+                pltpu.make_async_copy(ref.at[:, :, columns], hbm.at[:, :, columns], out_sems.at[n, i])
+            )
+            out_copies[-1].start()
+    for copy in out_copies:
+        copy.wait()
 
 
 def finish(attended, weights, tokens):
     return pl.pallas_call(
         finish_kernel,
         in_specs=[VMEM] + [HBM] * 6,
-        out_specs=(VMEM, VMEM),
+        out_specs=(HBM, HBM),
         out_shape=(
-            jax.ShapeDtypeStruct((WINDOWS, 16, D), F32),
+            jax.ShapeDtypeStruct((WINDOWS, 16, D), BF16),
             jax.ShapeDtypeStruct((WINDOWS, 16, D), BF16),
         ),
         scratch_shapes=[
@@ -267,7 +285,10 @@
             pltpu.VMEM((WINDOWS, 16, D), BF16),
             pltpu.VMEM((X_COUNT * GROUP // 128, PLANE * WINDOWS, 128), F32),
             pltpu.VMEM((PLANE * WINDOWS, X_COUNT * GROUP), BF16),
+            pltpu.VMEM((WINDOWS, 16, D), BF16),
+            pltpu.VMEM((WINDOWS, 16, D), BF16),
             pltpu.SemaphoreType.DMA((CHUNKS + 1, 10)),
+            pltpu.SemaphoreType.DMA((CHUNKS, 2)),
         ],
         compiler_params=pltpu.CompilerParams(vmem_limit_bytes=50 * 1024 * 1024),
         cost_estimate=pl.CostEstimate(flops=2 * 256 * 1280 * D, bytes_accessed=9_000_000, transcendentals=0),
@@ -289,9 +310,11 @@
         sent.reshape(X_COUNT * PLANE, 2 * WINDOWS, SLOT), ("x", "y", "z"), split_axis=0, concat_axis=0, tiled=True
     )
     attended = attend(received.reshape(X_COUNT, PLANE, 2, WINDOWS, SLOT))
-    returned = lax.all_to_all(attended, ("y", "z"), split_axis=0, concat_axis=0, tiled=True)
+    returned = lax.all_to_all(
+        attended.reshape(PLANE, WINDOWS, X_COUNT * GROUP), ("z", "y"), split_axis=0, concat_axis=0, tiled=True
+    )
     own, other = finish(returned, (w_out, w1, w2a, w2b, w3), tokens)
-    return (own + shift(other, "c", 1).astype(F32)).astype(BF16)
+    return (own.astype(F32) + shift(other, "c", 1).astype(F32)).astype(BF16)
 
 
 def solution(mesh):

time: 123 us -> 120 us (0.976)
  Pallas kernels: 20.4 us -> 18.9 us
  other arithmetic: 2.29 us -> 0.99 us
    convert_element_type x1, other arithmetic: 2.29 us -> 0.99 us  [local(): return (own.astype(F32) + shift(other, 'c', 1).astype(F32)).astype(BF16)]
where the time goes in v4:
time: 120 us; the launch traced here: 118 us
  waiting for transfers between devices  65.8 us (55%)
  starting transfers between devices  29.8 us (25%)
  Pallas kernels  18.9 us (16%)
  local copies, waits for them, and re-layouts  2.4 us (2%)
    all_to_all x1, waiting for transfers between devices, local(): lax.all_to_all(sent.reshape(X_COUNT * PLANE, 2 * WINDOWS, SLOT), ('x', 'y...  47.8 us
    ppermute x5, waiting for transfers between devices, shift(): lax.ppermute(value, axis, [(i, (i + by) % count) for i in range(count)])  17.9 us
    all_to_all x1, starting transfers between devices, local(): lax.all_to_all(sent.reshape(X_COUNT * PLANE, 2 * WINDOWS, SLOT), ('x', 'y...  15.4 us
    pallas_call x1, Pallas kernels, project(): pl.pallas_call(project_kernel, in_specs=[HBM, HBM, HBM, HBM], out_specs=H...  11.8 us
    all_to_all x1, starting transfers between devices, local(): lax.all_to_all(attended.reshape(PLANE, WINDOWS, X_COUNT * GROUP), ('z', '...  7.38 us
    ppermute x5, starting transfers between devices, shift(): lax.ppermute(value, axis, [(i, (i + by) % count) for i in range(count)])  7.08 us
    pallas_call x1, Pallas kernels, finish(): pl.pallas_call(finish_kernel, in_specs=[VMEM] + [HBM] * 6, out_specs=(HBM...  4.64 us
    pallas_call x1, Pallas kernels, attend(): pl.pallas_call(attend_kernel, in_specs=[VMEM], out_specs=VMEM, out_shape=...  2.51 us
  transfers between devices with their start and end apart: 7, of which 4 were waited for; matrix products, arithmetic and copies ran while one was open for 2% of the time, Pallas kernels for 2%

profile of v4, /device:TPU:8, one launch (start us, length us, event | category | flops | bytes accessed | tf_op | source)
XLA Modules:
  0.0 118.0 jit_solution(14895024357256989103)
XLA Ops:
  0.0 11.8 %shard_map.55 = bf16[128,2,8,512]{3,2,1,0:T(8,128)(2,1)} custom-call(bf16[8,128,2560]{2,1,0:T(8,128)(2,1)} %tokens_hbm.3, s32[8,128]{1,0:T(8,128)} %keep_hbm.1, f32[2560]{0:T(1024)} %gain_hbm.1, bf16[3,2,160,2560]{3,2,1,0:T(8,128)(2,1)} %bitcast.14), custom_call_target="tpu_custom_call" | custom-call | flops 5368709120 | bytes 14000000 | tf_op jit(solution)/shard_map/pallas_call | solution.py:127
  11.8 15.4 %all-to-all-start = ((bf16[128,16,512]{2,1,0:T(8,128)(2,1)}), bf16[128,16,512]{2,1,0:T(8,128)(2,1)S(1)}, u32[]{:S(2)}, u32[]{:S(2)}) async-start(bf16[128,16,512]{2,1,0:T(8,128)(2,1)} %bitcast.12), calls=%async_computation | async-start | bytes 4194304 | tf_op jit(solution)/shard_map/all_to_all | solution.py:309
  27.2 1.7 %collective-permute-start = (bf16[320,2560]{1,0:T(8,128)(2,1)}, bf16[320,2560]{1,0:T(8,128)(2,1)}, u32[]{:S(2)}, u32[]{:S(2)}) collective-permute-start(bf16[320,2560]{1,0:T(8,128)(2,1)} %param.9), channel_id=1, source_target_pairs={{0,2},{2,4},{4,6},{6,0},{1,3},{3,5},{5,7},{7,1},{8,10},{10,12},{12... | collective-permute-start | bytes 4915208 | tf_op jit(solution)/shard_map/ppermute | solution.py:300
  28.9 1.9 %collective-permute-start.2 = (bf16[320,2560]{1,0:T(8,128)(2,1)}, bf16[320,2560]{1,0:T(8,128)(2,1)}, u32[]{:S(2)}, u32[]{:S(2)}) collective-permute-start(bf16[320,2560]{1,0:T(8,128)(2,1)} %param.9), channel_id=1, source_target_pairs={{0,6},{2,0},{4,2},{6,4},{1,7},{3,1},{5,3},{7,5},{8,14},{10,8},{12,... | collective-permute-start | bytes 4915208 | tf_op jit(solution)/shard_map/ppermute | solution.py:300
  30.8 47.8 %all-to-all-done = bf16[128,16,512]{2,1,0:T(8,128)(2,1)S(1)} async-done(((bf16[128,16,512]{2,1,0:T(8,128)(2,1)}), bf16[128,16,512]{2,1,0:T(8,128)(2,1)S(1)}, u32[]{:S(2)}, u32[]{:S(2)}) %all-to-all-start) | async-done | bytes 2097184 | tf_op jit(solution)/shard_map/all_to_all | solution.py:309
  78.6 2.5 %shard_map.56 = bf16[8,4,8,1280]{3,2,1,0:T(8,128)(2,1)} custom-call(bf16[4,32,2,8,512]{4,3,2,1,0:T(8,128)(2,1)S(1)} %bitcast.9), custom_call_target="tpu_custom_call" | custom-call | flops 536870912 | bytes 2800000 | tf_op jit(solution)/shard_map/pallas_call | solution.py:202
  81.1 7.4 %all-to-all-start.1 = ((bf16[32,8,1280]{2,1,0:T(8,128)(2,1)}), bf16[32,8,1280]{2,1,0:T(8,128)(2,1)S(1)}, u32[]{:S(2)}, u32[]{:S(2)}) async-start(bf16[32,8,1280]{2,1,0:T(8,128)(2,1)} %bitcast.3), calls=%async_computation.1 | async-start | bytes 1310720 | tf_op jit(solution)/shard_map/all_to_all | solution.py:313
  88.5 0.0 collective-permute-done
  88.5 1.2 %slice.8 = bf16[160,2560]{1,0:T(8,128)(2,1)S(1)} slice(bf16[320,2560]{1,0:T(8,128)(2,1)} %collective-permute-done), slice={[0:160], [0:2560]} | slice | bytes 1638400 | tf_op jit(solution)/shard_map/slice | solution.py:306
  89.7 0.1 collective-permute-start.1
  89.8 0.0 collective-permute-done.2
  89.8 1.2 %slice.9 = bf16[160,2560]{1,0:T(8,128)(2,1)S(1)} slice(bf16[320,2560]{1,0:T(8,128)(2,1)} %collective-permute-done.2), slice={[160:320], [0:2560]} | slice | bytes 1638400 | tf_op jit(solution)/shard_map/slice | solution.py:307
  91.0 3.3 %collective-permute-start.3 = (bf16[160,2560]{1,0:T(8,128)(2,1)S(1)}, bf16[160,2560]{1,0:T(8,128)(2,1)S(1)}, u32[]{:S(2)}, u32[]{:S(2)}) collective-permute-start(bf16[160,2560]{1,0:T(8,128)(2,1)S(1)} %slice.9), channel_id=1, source_target_pairs={{0,6},{2,0},{4,2},{6,4},{1,7},{3,1},{5,3},{7,5},{8,14},{10,8},{12,... | collective-permute-start | bytes 2457608 | tf_op jit(solution)/shard_map/ppermute | solution.py:300
  94.3 15.3 %collective-permute-done.1 = bf16[160,2560]{1,0:T(8,128)(2,1)S(1)} collective-permute-done((bf16[160,2560]{1,0:T(8,128)(2,1)S(1)}, bf16[160,2560]{1,0:T(8,128)(2,1)S(1)}, u32[]{:S(2)}, u32[]{:S(2)}) %collective-permute-start.1) | collective-permute-done | bytes 819232 | tf_op jit(solution)/shard_map/ppermute | solution.py:300
  109.6 0.5 collective-permute-done.3
  110.2 0.0 all-to-all-done.1.attended_ref
  110.2 4.6 %shard_map.57 = (bf16[8,16,2560]{2,1,0:T(8,128)(2,1)S(1)}, bf16[8,16,2560]{2,1,0:T(8,128)(2,1)S(1)}) custom-call(bf16[32,8,1280]{2,1,0:T(8,128)(2,1)S(1)} %all-to-all-done.1.attended_ref, bf16[2,160,2560]{2,1,0:T(8,128)(2,1)} %bitcast.13, bf16[2,160,2560]{2,1,0:T(8,128)(2,1)} %bitcast.5.w1, bf16[1,160,2560]{2,1,0:T(8,128)(2,1)S(1)} %bitcast.10, ...), custom_call_target="tpu_custom_call" | custom-call | flops 1677721600 | bytes 9000000 | tf_op jit(solution)/shard_map/pallas_call | solution.py:274
  114.8 0.1 collective-permute-start.4
  114.9 2.1 %collective-permute-done.4 = bf16[8,16,2560]{2,1,0:T(8,128)(2,1)S(1)} collective-permute-done((bf16[8,16,2560]{2,1,0:T(8,128)(2,1)S(1)}, bf16[8,16,2560]{2,1,0:T(8,128)(2,1)S(1)}, u32[]{:S(2)}, u32[]{:S(2)}) %collective-permute-start.4) | collective-permute-done | bytes 655392 | tf_op jit(solution)/shard_map/ppermute | solution.py:300
  117.0 1.0 add_convert_fusion
Async XLA Ops:
  11.8 66.8 %all-to-all-start = ((bf16[128,16,512]{2,1,0:T(8,128)(2,1)}), bf16[128,16,512]{2,1,0:T(8,128)(2,1)S(1)}, u32[]{:S(2)}, u32[]{:S(2)}) async-start(bf16[128,16,512]{2,1,0:T(8,128)(2,1)} %bitcast.12), calls=%async_computation | async-start | bytes 4194304 | tf_op jit(solution)/shard_map/all_to_all | solution.py:309
  27.2 61.4 %collective-permute-start = (bf16[320,2560]{1,0:T(8,128)(2,1)}, bf16[320,2560]{1,0:T(8,128)(2,1)}, u32[]{:S(2)}, u32[]{:S(2)}) collective-permute-start(bf16[320,2560]{1,0:T(8,128)(2,1)} %param.9), channel_id=1, source_target_pairs={{0,2},{2,4},{4,6},{6,0},{1,3},{3,5},{5,7},{7,1},{8,10},{10,12},{12... | collective-permute-start | bytes 4915208 | tf_op jit(solution)/shard_map/ppermute | solution.py:300
  28.9 61.0 %collective-permute-start.2 = (bf16[320,2560]{1,0:T(8,128)(2,1)}, bf16[320,2560]{1,0:T(8,128)(2,1)}, u32[]{:S(2)}, u32[]{:S(2)}) collective-permute-start(bf16[320,2560]{1,0:T(8,128)(2,1)} %param.9), channel_id=1, source_target_pairs={{0,6},{2,0},{4,2},{6,4},{1,7},{3,1},{5,3},{7,5},{8,14},{10,8},{12,... | collective-permute-start | bytes 4915208 | tf_op jit(solution)/shard_map/ppermute | solution.py:300
  81.1 29.0 %all-to-all-start.1 = ((bf16[32,8,1280]{2,1,0:T(8,128)(2,1)}), bf16[32,8,1280]{2,1,0:T(8,128)(2,1)S(1)}, u32[]{:S(2)}, u32[]{:S(2)}) async-start(bf16[32,8,1280]{2,1,0:T(8,128)(2,1)} %bitcast.3), calls=%async_computation.1 | async-start | bytes 1310720 | tf_op jit(solution)/shard_map/all_to_all | solution.py:313
  89.7 19.9 %collective-permute-start.1 = (bf16[160,2560]{1,0:T(8,128)(2,1)S(1)}, bf16[160,2560]{1,0:T(8,128)(2,1)S(1)}, u32[]{:S(2)}, u32[]{:S(2)}) collective-permute-start(bf16[160,2560]{1,0:T(8,128)(2,1)S(1)} %slice.8), channel_id=1, source_target_pairs={{0,2},{2,4},{4,6},{6,0},{1,3},{3,5},{5,7},{7,1},{8,10},{10,12},{12... | collective-permute-start | bytes 2457608 | tf_op jit(solution)/shard_map/ppermute | solution.py:300
  91.0 19.1 %collective-permute-start.3 = (bf16[160,2560]{1,0:T(8,128)(2,1)S(1)}, bf16[160,2560]{1,0:T(8,128)(2,1)S(1)}, u32[]{:S(2)}, u32[]{:S(2)}) collective-permute-start(bf16[160,2560]{1,0:T(8,128)(2,1)S(1)} %slice.9), channel_id=1, source_target_pairs={{0,6},{2,0},{4,2},{6,4},{1,7},{3,1},{5,3},{7,5},{8,14},{10,8},{12,... | collective-permute-start | bytes 2457608 | tf_op jit(solution)/shard_map/ppermute | solution.py:300
  114.8 2.2 %collective-permute-start.4 = (bf16[8,16,2560]{2,1,0:T(8,128)(2,1)S(1)}, bf16[8,16,2560]{2,1,0:T(8,128)(2,1)S(1)}, u32[]{:S(2)}, u32[]{:S(2)}) collective-permute-start(bf16[8,16,2560]{2,1,0:T(8,128)(2,1)S(1)} %get-tuple-element.8), channel_id=1, source_target_pairs={{0,1},{1,0},{2,3},{3,2},{4,5},{5,4},{6,7},{7,6},{8,9},{9,8},{10,11... | collective-permute-start | bytes 1966088 | tf_op jit(solution)/shard_map/ppermute | solution.py:300

commit v5 on v4

--- a/solution.py
+++ b/solution.py
@@ -53,7 +53,7 @@
     out_copies = [
         [
             pltpu.make_async_copy(
-                out_ref.at[pl.ds(b * BLOCK, BLOCK), h], out_hbm.at[pl.ds(b * BLOCK, BLOCK), h], sems.at[b, 1 + h]
+                out_ref.at[:, b, h], out_hbm.at[:, b, h], sems.at[b, 1 + h]
             )
             for h in range(2)
         ]
@@ -113,7 +113,7 @@
                     piece = jnp.where(
                         lane == FLAG, odd, jnp.where(lane == FLAG + 1, 1.0 - odd, piece)
                     )
-                out_ref[b * BLOCK:(b + 1) * BLOCK, h, :, lanes] = jnp.swapaxes(
+                out_ref[:, b, h, :, lanes] = jnp.swapaxes(
                     piece.reshape(WINDOWS, BLOCK, 128), 0, 1
                 ).astype(BF16)
             out_copies[b][h].start()
@@ -128,9 +128,9 @@
         project_kernel,
         in_specs=[HBM, HBM, HBM, HBM],
         out_specs=HBM,
-        out_shape=jax.ShapeDtypeStruct((PAIRS, 2, WINDOWS, SLOT), BF16),
+        out_shape=jax.ShapeDtypeStruct((PLANE, X_COUNT, 2, WINDOWS, SLOT), BF16),
         scratch_shapes=[
-            pltpu.VMEM((PAIRS, 2, WINDOWS, SLOT), BF16),
+            pltpu.VMEM((PLANE, X_COUNT, 2, WINDOWS, SLOT), BF16),
             pltpu.VMEM((D,), F32),
             pltpu.VMEM((BLOCKS, WINDOWS, BLOCK, D), BF16),
             pltpu.VMEM((WINDOWS, PAIRS), jnp.int32),
@@ -150,7 +150,7 @@
     total = PLANE * WINDOWS
     scale = 1.0 / math.sqrt(HEAD_DIM)
     lane = lax.broadcasted_iota(jnp.int32, (total, 128), 1)
-    flags = in_ref[0, :, 0, :, LAST:].astype(F32).reshape(total, 128)
+    flags = in_ref[:, 0, 0, :, LAST:].astype(F32).reshape(total, 128)
     flags = jnp.where(lane >= FLAG, flags, 0.0).astype(BF16)
     same = lax.dot_general(flags, flags, (((1,), (1,)), ((), ())), preferred_element_type=F32) > 0.5
     me = lax.axis_index("x")
@@ -169,7 +169,7 @@
             source = lax.rem(me - d + X_COUNT, X_COUNT)
 
             def part(i):
-                return in_ref[source, :, h, :, i * 128:(i + 1) * 128].astype(F32).reshape(total, 128)
+                return in_ref[:, source, h, :, i * 128:(i + 1) * 128].astype(F32).reshape(total, 128)
 
             last = part(3)
             query = jnp.concatenate([part(0), jnp.where(lane < TAIL, last, 0.0)], axis=-1).astype(BF16)
@@ -307,9 +307,9 @@
     w2b = shift(w3[HEAD_DIM:], "x", -1)
     sent = project(tokens, keep_index, norm_gain, w_qkv)
     received = lax.all_to_all(
-        sent.reshape(X_COUNT * PLANE, 2 * WINDOWS, SLOT), ("x", "y", "z"), split_axis=0, concat_axis=0, tiled=True
+        sent.reshape(X_COUNT * PLANE, 2 * WINDOWS, SLOT), ("y", "z", "x"), split_axis=0, concat_axis=0, tiled=True
     )
-    attended = attend(received.reshape(X_COUNT, PLANE, 2, WINDOWS, SLOT))
+    attended = attend(received.reshape(PLANE, X_COUNT, 2, WINDOWS, SLOT))
     returned = lax.all_to_all(
         attended.reshape(PLANE, WINDOWS, X_COUNT * GROUP), ("z", "y"), split_axis=0, concat_axis=0, tiled=True
     )

time: 120 us -> 120 us (level)
  starting transfers between devices: 29.8 us -> 27.7 us
  waiting for transfers between devices: 65.8 us -> 67.7 us
    all_to_all x1, starting transfers between devices: 7.38 us -> 5.41 us  [local(): lax.all_to_all(attended.reshape(PLANE, WINDOWS, X_COUNT * GROUP), ('z', '...]
where the time goes in v5:
time: 120 us; the launch traced here: 118 us
  waiting for transfers between devices  67.7 us (56%)
  starting transfers between devices  27.7 us (23%)
  Pallas kernels  19 us (16%)
  local copies, waits for them, and re-layouts  2.4 us (2%)
    all_to_all x1, waiting for transfers between devices, local(): lax.all_to_all(sent.reshape(X_COUNT * PLANE, 2 * WINDOWS, SLOT), ('y', 'z...  48.7 us
    ppermute x5, waiting for transfers between devices, shift(): lax.ppermute(value, axis, [(i, (i + by) % count) for i in range(count)])  19 us
    all_to_all x1, starting transfers between devices, local(): lax.all_to_all(sent.reshape(X_COUNT * PLANE, 2 * WINDOWS, SLOT), ('y', 'z...  15.5 us
    pallas_call x1, Pallas kernels, project(): pl.pallas_call(project_kernel, in_specs=[HBM, HBM, HBM, HBM], out_specs=H...  11.8 us
    ppermute x5, starting transfers between devices, shift(): lax.ppermute(value, axis, [(i, (i + by) % count) for i in range(count)])  6.8 us
    all_to_all x1, starting transfers between devices, local(): lax.all_to_all(attended.reshape(PLANE, WINDOWS, X_COUNT * GROUP), ('z', '...  5.41 us
    pallas_call x1, Pallas kernels, finish(): pl.pallas_call(finish_kernel, in_specs=[VMEM] + [HBM] * 6, out_specs=(HBM...  4.64 us
    pallas_call x1, Pallas kernels, attend(): pl.pallas_call(attend_kernel, in_specs=[VMEM], out_specs=VMEM, out_shape=...  2.51 us
  transfers between devices with their start and end apart: 7, of which 4 were waited for; matrix products, arithmetic and copies ran while one was open for 2% of the time, Pallas kernels for 2%

profile of v5, /device:TPU:8, one launch (start us, length us, event | category | flops | bytes accessed | tf_op | source)
XLA Modules:
  0.0 117.7 jit_solution(3182804637689104190)
XLA Ops:
  0.0 11.8 %shard_map.55 = bf16[32,4,2,8,512]{4,3,2,1,0:T(8,128)(2,1)} custom-call(bf16[8,128,2560]{2,1,0:T(8,128)(2,1)} %tokens_hbm.3, s32[8,128]{1,0:T(8,128)} %keep_hbm.1, f32[2560]{0:T(1024)} %gain_hbm.1, bf16[3,2,160,2560]{3,2,1,0:T(8,128)(2,1)} %bitcast.14), custom_call_target="tpu_custom_call" | custom-call | flops 5368709120 | bytes 14000000 | tf_op jit(solution)/shard_map/pallas_call | solution.py:127
  11.8 15.5 %all-to-all-start = ((bf16[128,16,512]{2,1,0:T(8,128)(2,1)}), bf16[128,16,512]{2,1,0:T(8,128)(2,1)S(1)}, u32[]{:S(2)}, u32[]{:S(2)}) async-start(bf16[128,16,512]{2,1,0:T(8,128)(2,1)} %bitcast.12), calls=%async_computation | async-start | bytes 4194304 | tf_op jit(solution)/shard_map/all_to_all | solution.py:309
  27.3 1.5 %collective-permute-start = (bf16[320,2560]{1,0:T(8,128)(2,1)}, bf16[320,2560]{1,0:T(8,128)(2,1)}, u32[]{:S(2)}, u32[]{:S(2)}) collective-permute-start(bf16[320,2560]{1,0:T(8,128)(2,1)} %param.9), channel_id=1, source_target_pairs={{0,2},{2,4},{4,6},{6,0},{1,3},{3,5},{5,7},{7,1},{8,10},{10,12},{12... | collective-permute-start | bytes 4915208 | tf_op jit(solution)/shard_map/ppermute | solution.py:300
  28.8 1.8 %collective-permute-start.2 = (bf16[320,2560]{1,0:T(8,128)(2,1)}, bf16[320,2560]{1,0:T(8,128)(2,1)}, u32[]{:S(2)}, u32[]{:S(2)}) collective-permute-start(bf16[320,2560]{1,0:T(8,128)(2,1)} %param.9), channel_id=1, source_target_pairs={{0,6},{2,0},{4,2},{6,4},{1,7},{3,1},{5,3},{7,5},{8,14},{10,8},{12,... | collective-permute-start | bytes 4915208 | tf_op jit(solution)/shard_map/ppermute | solution.py:300
  30.6 48.7 %all-to-all-done = bf16[128,16,512]{2,1,0:T(8,128)(2,1)S(1)} async-done(((bf16[128,16,512]{2,1,0:T(8,128)(2,1)}), bf16[128,16,512]{2,1,0:T(8,128)(2,1)S(1)}, u32[]{:S(2)}, u32[]{:S(2)}) %all-to-all-start) | async-done | bytes 2097184 | tf_op jit(solution)/shard_map/all_to_all | solution.py:309
  79.3 2.5 %shard_map.56 = bf16[8,4,8,1280]{3,2,1,0:T(8,128)(2,1)} custom-call(bf16[32,4,2,8,512]{4,3,2,1,0:T(8,128)(2,1)S(1)} %bitcast.9), custom_call_target="tpu_custom_call" | custom-call | flops 536870912 | bytes 2800000 | tf_op jit(solution)/shard_map/pallas_call | solution.py:202
  81.8 5.4 %all-to-all-start.1 = ((bf16[32,8,1280]{2,1,0:T(8,128)(2,1)}), bf16[32,8,1280]{2,1,0:T(8,128)(2,1)S(1)}, u32[]{:S(2)}, u32[]{:S(2)}) async-start(bf16[32,8,1280]{2,1,0:T(8,128)(2,1)} %bitcast.3), calls=%async_computation.1 | async-start | bytes 1310720 | tf_op jit(solution)/shard_map/all_to_all | solution.py:313
  87.2 0.0 collective-permute-done
  87.2 1.2 %slice.8 = bf16[160,2560]{1,0:T(8,128)(2,1)S(1)} slice(bf16[320,2560]{1,0:T(8,128)(2,1)} %collective-permute-done), slice={[0:160], [0:2560]} | slice | bytes 1638400 | tf_op jit(solution)/shard_map/slice | solution.py:306
  88.4 0.6 collective-permute-start.1
  89.0 0.0 collective-permute-done.2
  89.0 1.2 %slice.9 = bf16[160,2560]{1,0:T(8,128)(2,1)S(1)} slice(bf16[320,2560]{1,0:T(8,128)(2,1)} %collective-permute-done.2), slice={[160:320], [0:2560]} | slice | bytes 1638400 | tf_op jit(solution)/shard_map/slice | solution.py:307
  90.2 2.8 %collective-permute-start.3 = (bf16[160,2560]{1,0:T(8,128)(2,1)S(1)}, bf16[160,2560]{1,0:T(8,128)(2,1)S(1)}, u32[]{:S(2)}, u32[]{:S(2)}) collective-permute-start(bf16[160,2560]{1,0:T(8,128)(2,1)S(1)} %slice.9), channel_id=1, source_target_pairs={{0,6},{2,0},{4,2},{6,4},{1,7},{3,1},{5,3},{7,5},{8,14},{10,8},{12,... | collective-permute-start | bytes 2457608 | tf_op jit(solution)/shard_map/ppermute | solution.py:300
  93.0 16.3 %collective-permute-done.1 = bf16[160,2560]{1,0:T(8,128)(2,1)S(1)} collective-permute-done((bf16[160,2560]{1,0:T(8,128)(2,1)S(1)}, bf16[160,2560]{1,0:T(8,128)(2,1)S(1)}, u32[]{:S(2)}, u32[]{:S(2)}) %collective-permute-start.1) | collective-permute-done | bytes 819232 | tf_op jit(solution)/shard_map/ppermute | solution.py:300
  109.4 0.5 collective-permute-done.3
  109.9 0.0 all-to-all-done.1.attended_ref
  109.9 4.6 %shard_map.57 = (bf16[8,16,2560]{2,1,0:T(8,128)(2,1)S(1)}, bf16[8,16,2560]{2,1,0:T(8,128)(2,1)S(1)}) custom-call(bf16[32,8,1280]{2,1,0:T(8,128)(2,1)S(1)} %all-to-all-done.1.attended_ref, bf16[2,160,2560]{2,1,0:T(8,128)(2,1)} %bitcast.13, bf16[2,160,2560]{2,1,0:T(8,128)(2,1)} %bitcast.5.w1, bf16[1,160,2560]{2,1,0:T(8,128)(2,1)S(1)} %bitcast.10, ...), custom_call_target="tpu_custom_call" | custom-call | flops 1677721600 | bytes 9000000 | tf_op jit(solution)/shard_map/pallas_call | solution.py:274
  114.6 0.1 collective-permute-start.4
  114.7 2.1 %collective-permute-done.4 = bf16[8,16,2560]{2,1,0:T(8,128)(2,1)S(1)} collective-permute-done((bf16[8,16,2560]{2,1,0:T(8,128)(2,1)S(1)}, bf16[8,16,2560]{2,1,0:T(8,128)(2,1)S(1)}, u32[]{:S(2)}, u32[]{:S(2)}) %collective-permute-start.4) | collective-permute-done | bytes 655392 | tf_op jit(solution)/shard_map/ppermute | solution.py:300
  116.7 1.0 add_convert_fusion
Async XLA Ops:
  11.8 67.5 %all-to-all-start = ((bf16[128,16,512]{2,1,0:T(8,128)(2,1)}), bf16[128,16,512]{2,1,0:T(8,128)(2,1)S(1)}, u32[]{:S(2)}, u32[]{:S(2)}) async-start(bf16[128,16,512]{2,1,0:T(8,128)(2,1)} %bitcast.12), calls=%async_computation | async-start | bytes 4194304 | tf_op jit(solution)/shard_map/all_to_all | solution.py:309
  27.3 60.0 %collective-permute-start = (bf16[320,2560]{1,0:T(8,128)(2,1)}, bf16[320,2560]{1,0:T(8,128)(2,1)}, u32[]{:S(2)}, u32[]{:S(2)}) collective-permute-start(bf16[320,2560]{1,0:T(8,128)(2,1)} %param.9), channel_id=1, source_target_pairs={{0,2},{2,4},{4,6},{6,0},{1,3},{3,5},{5,7},{7,1},{8,10},{10,12},{12... | collective-permute-start | bytes 4915208 | tf_op jit(solution)/shard_map/ppermute | solution.py:300
  28.8 60.2 %collective-permute-start.2 = (bf16[320,2560]{1,0:T(8,128)(2,1)}, bf16[320,2560]{1,0:T(8,128)(2,1)}, u32[]{:S(2)}, u32[]{:S(2)}) collective-permute-start(bf16[320,2560]{1,0:T(8,128)(2,1)} %param.9), channel_id=1, source_target_pairs={{0,6},{2,0},{4,2},{6,4},{1,7},{3,1},{5,3},{7,5},{8,14},{10,8},{12,... | collective-permute-start | bytes 4915208 | tf_op jit(solution)/shard_map/ppermute | solution.py:300
  81.8 28.1 %all-to-all-start.1 = ((bf16[32,8,1280]{2,1,0:T(8,128)(2,1)}), bf16[32,8,1280]{2,1,0:T(8,128)(2,1)S(1)}, u32[]{:S(2)}, u32[]{:S(2)}) async-start(bf16[32,8,1280]{2,1,0:T(8,128)(2,1)} %bitcast.3), calls=%async_computation.1 | async-start | bytes 1310720 | tf_op jit(solution)/shard_map/all_to_all | solution.py:313
  88.4 20.9 %collective-permute-start.1 = (bf16[160,2560]{1,0:T(8,128)(2,1)S(1)}, bf16[160,2560]{1,0:T(8,128)(2,1)S(1)}, u32[]{:S(2)}, u32[]{:S(2)}) collective-permute-start(bf16[160,2560]{1,0:T(8,128)(2,1)S(1)} %slice.8), channel_id=1, source_target_pairs={{0,2},{2,4},{4,6},{6,0},{1,3},{3,5},{5,7},{7,1},{8,10},{10,12},{12... | collective-permute-start | bytes 2457608 | tf_op jit(solution)/shard_map/ppermute | solution.py:300
  90.2 19.7 %collective-permute-start.3 = (bf16[160,2560]{1,0:T(8,128)(2,1)S(1)}, bf16[160,2560]{1,0:T(8,128)(2,1)S(1)}, u32[]{:S(2)}, u32[]{:S(2)}) collective-permute-start(bf16[160,2560]{1,0:T(8,128)(2,1)S(1)} %slice.9), channel_id=1, source_target_pairs={{0,6},{2,0},{4,2},{6,4},{1,7},{3,1},{5,3},{7,5},{8,14},{10,8},{12,... | collective-permute-start | bytes 2457608 | tf_op jit(solution)/shard_map/ppermute | solution.py:300
  114.6 2.2 %collective-permute-start.4 = (bf16[8,16,2560]{2,1,0:T(8,128)(2,1)S(1)}, bf16[8,16,2560]{2,1,0:T(8,128)(2,1)S(1)}, u32[]{:S(2)}, u32[]{:S(2)}) collective-permute-start(bf16[8,16,2560]{2,1,0:T(8,128)(2,1)S(1)} %get-tuple-element.8), channel_id=1, source_target_pairs={{0,1},{1,0},{2,3},{3,2},{4,5},{5,4},{6,7},{7,6},{8,9},{9,8},{10,11... | collective-permute-start | bytes 1966088 | tf_op jit(solution)/shard_map/ppermute | solution.py:300
